TPU v7x, 32 devices: a whole 2x2x4 slice. The times are simulated.
32 devices in a mesh: dp: 4 (over y, x), pts: 8 (over z, core).
Axes of the slice: x: 2, y: 2, z: 4, core: 2. Of those that a mesh axis runs over, the one named last changes fastest.
Arguments:
- features: bfloat16 [32768, 256], P(('dp', 'pts')), parts along dimension 0, may hold values from -6 to 6
- tile_slot: int32 [32768], P(('dp', 'pts')), parts along dimension 0, may hold values from 0 to 16383, as said below
- neighbors: int32 [27, 65536], P(None, ('dp', 'pts')), parts along dimension 1, may hold values from 0 to 2304, as said below
- serial: int32 [65536], P(('dp', 'pts')), parts along dimension 0, may hold values from -1 to 8191, as said below
- conv_weight: bfloat16 [27, 256, 256], replicated, may hold values from -0.078125 to 0.078125
- conv_bias: float32 [256], replicated, may hold values from -3 to 3
- cpe_gain: float32 [256], replicated, may hold values from 0.1 to 1.9
- cpe_bias: float32 [256], replicated, may hold values from -3 to 3
- norm_gain: float32 [256], replicated, may hold values from 0.1 to 1.9
- norm_bias: float32 [256], replicated, may hold values from -3 to 3
- qkv_weight: bfloat16 [256, 768], replicated, may hold values from -0.375 to 0.375
- qkv_bias: float32 [768], replicated, may hold values from -50 to 50
- proj_weight: bfloat16 [256, 256], replicated, may hold values from -0.375 to 0.375
- proj_bias: float32 [256], replicated, may hold values from -3 to 3
Outputs:
- output: bfloat16 [32768, 256], P(('dp', 'pts')), parts along dimension 0
There are 4 independent parts, one for each index of `dp`. A program takes and returns all parts, laid end to end along the dimension named above; an argument that names none is the same for every part. Nothing has to cross between parts.
Inputs may be any that keep to these rules, and one draw needn't show every extreme that they name: `tile_slot`: element i gives point i's owner (value // 2048) and slot (value % 2048); values are distinct. An owner holds a first run of its slots and always its last 128 slots; it holds at least 256 slots and some owner holds all 2048. From the 1024 points of one device at most 272 go to one owner, and some device sends exactly 272 to some owner. `neighbors`: entry [k, s] refers to the extended rows of slot s's owner: 0 to 127 are the last 128 slots of the owner before, 128 + j is the owner's own slot j, 2176 + j is slot j of the owner after, 2304 means no neighbour. Entries name held slots only; the first owner never names an owner before and the last none after. Entry 13 of a held slot is the slot itself; all entries of slots no point holds are 2304. `serial`: held slots carry the places 0 to 8191, each once; slots no point holds carry -1. From one owner at most 272 points go to the places of one device (block of 1024 places), and some owner sends exactly 272 to some device.
All inputs are finite; a program needn't handle non-finite values.
Results may differ from a plain program's by a relative error of at most 0.014.
Values may be sent and summed in bfloat16 or wider, within the bound.
A program may use at most 64 MiB of HBM per device.

v0:
```python
import jax
import jax.numpy as jnp
from jax import lax
from jax.sharding import PartitionSpec as P

HEADS = 16
HD = 16
PATCH = 1024
PTS_DEV = 1024
OWN_CAP = 2048
HALO = 128


EPSILON = 1e-05


def with_halo(shard, sides, width):
    for axis, dim in sides:
        size, length = (lax.axis_size(axis), shard.shape[dim])
        up = [(i, (i + 1) % size) for i in range(size - 1)]
        down = [(j, i) for i, j in up]
        last = lax.slice_in_dim(shard, length - width, length, axis=dim)
        initial = lax.slice_in_dim(shard, 0, width, axis=dim)
        before = lax.ppermute(last, axis, up)
        after = lax.ppermute(initial, axis, down)
        shard = jnp.concatenate([before, shard, after], axis=dim)
    return shard


def layer_norm(values, gain_vec, shift_vec):
    average = jnp.mean(values, axis=-1, keepdims=True)
    centred = values - average
    spread = jnp.mean(centred * centred, axis=-1, keepdims=True)
    return centred * lax.rsqrt(spread + EPSILON) * gain_vec + shift_vec


def arrival_rank(targets, wanted, num_peers):
    row_count = targets.shape[0]
    onehot = jnp.logical_and(targets[:, None] == jnp.arange(num_peers)[None, :], wanted[:, None])
    onehot_bf = onehot.astype(jnp.bfloat16)
    line = jnp.arange(row_count)
    lower = (line[None, :] < line[:, None]).astype(jnp.bfloat16)
    earlier = jnp.dot(lower, onehot_bf, preferred_element_type=jnp.float32)
    return jnp.sum(earlier * onehot.astype(jnp.float32), axis=1).astype(jnp.int32)


def buffer_index(targets, wanted, num_peers, stride, offset_in, overflow):
    ranking = arrival_rank(targets, wanted, num_peers)
    return jnp.where(wanted, targets * stride + offset_in + ranking, overflow)


def invert_index(where_to, count):
    block_rows = 512
    num_blocks = (count + block_rows - 1) // block_rows
    wanted_all = jnp.arange(num_blocks * block_rows, dtype=jnp.int32).reshape(
        num_blocks, block_rows
    )
    source_line = jnp.arange(where_to.shape[0], dtype=jnp.int32)

    def one_block(wanted_block):
        match = wanted_block[:, None] == where_to[None, :]
        source = jnp.sum(jnp.where(match, source_line[None, :], 0), axis=1)
        return (source, jnp.any(match, axis=1))

    source, found = lax.map(one_block, wanted_all)
    return (source.reshape(-1)[:count], found.reshape(-1)[:count])


def pick_rows(rows, source, found):
    return jnp.where(found[:, None], rows[source], jnp.zeros((), rows.dtype))


def attend(qkv_rows, model_width):
    local_rows = qkv_rows.shape[0]
    patches = local_rows // PATCH

    def split_heads(matrix):
        return matrix.reshape(patches, PATCH, HEADS, HD).transpose(2, 0, 1, 3)

    query_heads = split_heads(qkv_rows[:, :model_width])
    key_heads = split_heads(qkv_rows[:, model_width : 2 * model_width])
    value_heads = split_heads(qkv_rows[:, 2 * model_width :])

    def one_head(triple):
        query_h, key_h, value_h = triple
        scores = jnp.einsum(
            "pqd,pkd->pqk", query_h, key_h, preferred_element_type=jnp.float32
        ) * HD ** (-0.5)
        row_max = jnp.max(scores, axis=-1, keepdims=True)
        lifted = jnp.exp(scores - row_max)
        row_sum = jnp.sum(lifted, axis=-1, keepdims=True)
        weights = (lifted / row_sum).astype(jnp.bfloat16)
        return jnp.einsum(
            "pqk,pkd->pqd", weights, value_h, preferred_element_type=jnp.float32
        ).astype(jnp.bfloat16)

    heads_out = lax.map(one_head, (query_heads, key_heads, value_heads))
    return heads_out.transpose(1, 2, 0, 3).reshape(local_rows, model_width)


def body(
    features,
    tile_slot,
    neighbors,
    serial,
    conv_weight,
    conv_bias,
    cpe_gain,
    cpe_bias,
    norm_gain,
    norm_bias,
    qkv_weight,
    qkv_bias,
    proj_weight,
    proj_bias,
):
    num_peers = lax.axis_size("pts")
    local_rows = features.shape[0]
    model_width = features.shape[1]
    send_cap = 17 * local_rows // (8 * num_peers)
    owners = tile_slot // OWN_CAP
    slot_in = tile_slot % OWN_CAP
    all_rows = jnp.ones(owners.shape, dtype=bool)
    total_slots = num_peers * send_cap
    where_to = buffer_index(owners, all_rows, num_peers, send_cap, 0, total_slots)
    source, found = invert_index(where_to, total_slots)
    out_rows = pick_rows(features, source, found)
    out_slots = jnp.where(found, slot_in[source], OWN_CAP)
    got_rows, got_slots = (
        lax.all_to_all(
            out_rows.reshape(num_peers, send_cap, model_width),
            "pts",
            split_axis=0,
            concat_axis=0,
            tiled=True,
        ),
        lax.all_to_all(
            out_slots.reshape(num_peers, send_cap), "pts", split_axis=0, concat_axis=0, tiled=True
        ),
    )
    back, present = invert_index(got_slots.reshape(-1), OWN_CAP)
    tiled_rows = pick_rows(got_rows.reshape(-1, model_width), back, present)
    framed = with_halo(tiled_rows, (("pts", 0),), HALO)
    extended = jnp.concatenate([framed, jnp.zeros((1, model_width), jnp.bfloat16)], axis=0)
    row_block = 512
    tables = neighbors.reshape(27, OWN_CAP // row_block, row_block).transpose(1, 0, 2)

    def conv_block(lookup):
        pulled = extended[lookup]
        return jnp.einsum("kbd,kde->be", pulled, conv_weight, preferred_element_type=jnp.float32)

    conv_out = lax.map(conv_block, tables).reshape(OWN_CAP, model_width) + conv_bias
    hidden = (tiled_rows.astype(jnp.float32) + layer_norm(conv_out, cpe_gain, cpe_bias)).astype(
        jnp.bfloat16
    )
    placed_ok = serial >= 0
    devices_to = jnp.where(placed_ok, serial // PTS_DEV, 0)
    spot_in = serial % PTS_DEV
    total_out = num_peers * send_cap
    where_to = buffer_index(devices_to, placed_ok, num_peers, send_cap, 0, total_out)
    source, found = invert_index(where_to, total_out)
    sent_rows = pick_rows(hidden, source, found)
    sent_spots = jnp.where(found, spot_in[source], PTS_DEV)
    shaped = (
        sent_rows.reshape(num_peers, send_cap, model_width),
        sent_spots.reshape(num_peers, send_cap),
    )
    got_rows, got_spots = (
        lax.all_to_all(shaped[0], "pts", split_axis=0, concat_axis=0, tiled=True),
        lax.all_to_all(shaped[1], "pts", split_axis=0, concat_axis=0, tiled=True),
    )
    back, present = invert_index(got_spots.reshape(-1), local_rows)
    placed = pick_rows(got_rows.reshape(-1, model_width), back, present)
    normed = layer_norm(placed.astype(jnp.float32), norm_gain, norm_bias).astype(jnp.bfloat16)
    qkv_rows = (jnp.dot(normed, qkv_weight, preferred_element_type=jnp.float32) + qkv_bias).astype(
        jnp.bfloat16
    )
    attended = attend(qkv_rows, model_width)
    projected = jnp.dot(attended, proj_weight, preferred_element_type=jnp.float32) + proj_bias
    return (placed.astype(jnp.float32) + projected).astype(jnp.bfloat16)


def solution(mesh):
    placed = (
        P(("dp", "pts"), None),
        P(("dp", "pts")),
        P(None, ("dp", "pts")),
        P(("dp", "pts")),
        P(),
        P(),
        P(),
        P(),
        P(),
        P(),
        P(),
        P(),
        P(),
        P(),
    )
    return jax.shard_map(
        body, mesh=mesh, in_specs=placed, out_specs=P(("dp", "pts"), None), check_vma=False
    )
```

profile of v0, /device:TPU:0, one launch (start us, length us, event | category | flops | bytes accessed | tf_op | source)
XLA Modules:
  0.0 381.1 jit_solution(1665338282170055372)
XLA Ops:
  2.0 4.7 %while.77 = (s32[]{:T(128)}, s32[5,512]{1,0:T(8,128)S(1)}, pred[5,512]{1,0:T(8,128)(4,1)S(1)}, s32[5,512]{1,0:T(8,128)S(1)}, s32[1024]{0:T(1024)S(1)}, /*index=5*/s32[]{:T(128)}, s32[]{:T(128)}) while((s32[]{:T(128)}, s32[5,512]{1,0:T(8,128)S(1)}, pred[5,512]{1,0:T(8,128)(4,1)S(1)}, s32[5,512]{1,0:T(8,128)S(1)}, ...), condition=%wide.region_13.14_spmd.clone, body=%wide.region_10.13_spmd.clone.sunk | while | flops 2620418 | bytes 25177 | solution.py:65
  6.7 8.1 %gather_fusion.2 = s32[2176]{0:T(1024)S(1)} fusion(s32[1024]{0:T(1024)S(1)} %get-tuple-element.337, s32[3072]{0:T(1024)S(1)} %pad_clamp_fusion.1), kind=kCustom, calls=%fused_computation.2 | custom fusion | bytes 26112 | tf_op jit(solution)/shard_map/gather | solution.py:128
  15.5 6.3 %all-to-all-start.1 = ((s32[8,1,272]{2,1,0:T(1,128)}), s32[8,1,272]{2,1,0:T(1,128)S(1)}, u32[]{:S(2)}, u32[]{:S(2)}) async-start(s32[8,1,272]{2,1,0:T(1,128)} %select_n.142), calls=%async_computation.1 | async-start | bytes 24576 | tf_op jit(solution)/shard_map/all_to_all | solution.py:137
  21.9 7.1 %gather_fusion.3 = bf16[2176,256]{1,0:T(8,128)(2,1)S(1)} fusion(bf16[1024,256]{1,0:T(8,128)(2,1)S(1)} %copy-done, s32[3072]{0:T(1024)S(1)} %pad_clamp_fusion.1), kind=kCustom, calls=%fused_computation.3 | custom fusion | bytes 2236928 | tf_op jit(solution)/shard_map/gather | solution.py:70
  29.1 1.4 fusion.40
  30.5 7.6 %while.76 = (s32[]{:T(128)}, s32[5,512]{1,0:T(8,128)S(1)}, pred[5,512]{1,0:T(8,128)(4,1)S(1)}, s32[5,512]{1,0:T(8,128)S(1)}, s32[2048]{0:T(1024)S(1)}, /*index=5*/s32[]{:T(128)}, s32[]{:T(128)}) while((s32[]{:T(128)}, s32[5,512]{1,0:T(8,128)S(1)}, pred[5,512]{1,0:T(8,128)(4,1)S(1)}, s32[5,512]{1,0:T(8,128)S(1)}, ...), condition=%wide.region_4.5_spmd.clone, body=%wide.region_1.4_spmd.clone.sunk | while | flops 5241858 | bytes 33369 | solution.py:65
  38.2 1.3 broadcast_select_fusion
  39.5 11.7 %gather_fusion.1 = s32[2176]{0:T(1024)S(1)} fusion(s32[2048]{0:T(1024)S(1)} %get-tuple-element.333, s32[3072]{0:T(1024)S(1)} %pad_clamp_fusion.2), kind=kCustom, calls=%fused_computation.1 | custom fusion | bytes 26112 | tf_op jit(solution)/shard_map/gather | solution.py:163
  51.3 5.1 %all-to-all-start.2 = ((bf16[8,272,256]{2,1,0:T(8,128)(2,1)}), bf16[8,272,256]{2,1,0:T(8,128)(2,1)S(1)}, u32[]{:S(2)}, u32[]{:S(2)}) async-start(bf16[8,272,256]{2,1,0:T(8,128)(2,1)} %broadcast_select_fusion), calls=%async_computation.2 | async-start | bytes 2228224 | tf_op jit(solution)/shard_map/all_to_all | solution.py:130
  57.0 6.2 %while.79 = (s32[]{:T(128)}, s32[4,512]{1,0:T(4,128)S(1)}, pred[4,512]{1,0:T(4,128)(4,1)S(1)}, s32[4,512]{1,0:T(4,128)S(1)}, s32[8,272]{1,0:T(8,128)}, /*index=5*/s32[2176]{0:T(1024)S(1)}, s32[]{:T(128)}, s32[]{:T(128)}) while((s32[]{:T(128)}, s32[4,512]{1,0:T(4,128)S(1)}, pred[4,512]{1,0:T(4,128)(4,1)S(1)}, ...), condition=%wide.wide.region_17.18_spmd.clone, body=%wide.wide.region_14.17_spmd.clone.sunk | while | flops 5569538 | bytes 34401 | solution.py:65
  63.3 21.1 %all-to-all-done.2 = bf16[8,272,256]{2,1,0:T(8,128)(2,1)S(1)} async-done(((bf16[8,272,256]{2,1,0:T(8,128)(2,1)}), bf16[8,272,256]{2,1,0:T(8,128)(2,1)S(1)}, u32[]{:S(2)}, u32[]{:S(2)}) %all-to-all-start.2) | async-done | bytes 1114144 | tf_op jit(solution)/shard_map/all_to_all | solution.py:130
  84.3 7.5 %gather_fusion.4 = bf16[2048,256]{1,0:T(8,128)(2,1)S(1)} fusion(bf16[2176,256]{1,0:T(8,128)(2,1)S(1)} %bitcast.145, s32[2048]{0:T(1024)S(1)} %broadcast_clamp_fusion), kind=kCustom, calls=%fused_computation.4 | custom fusion | bytes 2105344 | tf_op jit(solution)/shard_map/gather | solution.py:70
  92.3 1.0 copy-done.2
  93.3 1.5 collective-permute-start
  94.9 1.3 collective-permute-start.1
  96.9 5.3 %all-to-all-start = ((s32[8,1,272]{2,1,0:T(1,128)}), s32[8,1,272]{2,1,0:T(1,128)S(1)}, u32[]{:S(2)}, u32[]{:S(2)}) async-start(s32[8,1,272]{2,1,0:T(1,128)} %select_n.137), calls=%async_computation | async-start | bytes 24576 | tf_op jit(solution)/shard_map/all_to_all | solution.py:170
  102.4 1.6 maximum_maximum_fusion
  104.1 182.8 %while.74 = (s32[]{:T(128)}, f32[4,512,256]{2,1,0:T(8,128)}, s32[4,27,512]{2,0,1:T(4,128)S(1)}, bf16[2305,256]{1,0:T(8,128)(2,1)S(1)}, bf16[27,256,256]{2,1,0:T(8,128)(2,1)}, /*index=5*/s32[]{:T(128)}) while((s32[]{:T(128)}, f32[4,512,256]{2,1,0:T(8,128)}, s32[4,27,512]{2,0,1:T(4,128)S(1)}, bf16[2305,256]{1,0:T(8,128)(2,1)S(1)}, ...), condition=%wide.region_19.20_spmd, body=%wide.region_18.19_spmd.sunk | while | flops 1811995136 | bytes 25797192 | solution.py:152
  104.2 38.8 %gather_fusion = bf16[13824,256]{1,0:T(8,128)(2,1)} fusion(bf16[2305,256]{1,0:T(8,128)(2,1)S(1)} %get-tuple-element.641, s32[14336]{0:T(1024)S(1)} %pad_clamp_fusion.4), kind=kCustom, calls=%fused_computation.clone.1 | custom fusion | bytes 14211072 | tf_op jit(solution)/shard_map/while/body/eval_jaxpr/gather | solution.py:149
  142.9 6.8 %fusion.84 = f32[4,512,256]{2,1,0:T(8,128)} fusion(f32[4,512,256]{2,1,0:T(8,128)} %get-tuple-element.633, s32[]{:T(128)} %get-tuple-element.632, bf16[27,512,256]{2,1,0:T(8,128)(2,1)} %bitcast.144, bf16[27,256,256]{2,1,0:T(8,128)(2,1)} %get-tuple-element.642), kind=kOutput, calls=%fused_computation.30.clone.1 | convolution fusion | flops 1811939328 | bytes 11141632 | tf_op jit(solution)/shard_map/while/body/eval_jaxpr/kbd,kde->be/dot_general | solution.py:150
  149.8 38.8 %gather_fusion = bf16[13824,256]{1,0:T(8,128)(2,1)} fusion(bf16[2305,256]{1,0:T(8,128)(2,1)S(1)} %get-tuple-element.641, s32[14336]{0:T(1024)S(1)} %pad_clamp_fusion.4), kind=kCustom, calls=%fused_computation.clone.1 | custom fusion | bytes 14211072 | tf_op jit(solution)/shard_map/while/body/eval_jaxpr/gather | solution.py:149
  188.6 6.8 %fusion.84 = f32[4,512,256]{2,1,0:T(8,128)} fusion(f32[4,512,256]{2,1,0:T(8,128)} %get-tuple-element.633, s32[]{:T(128)} %get-tuple-element.632, bf16[27,512,256]{2,1,0:T(8,128)(2,1)} %bitcast.144, bf16[27,256,256]{2,1,0:T(8,128)(2,1)} %get-tuple-element.642), kind=kOutput, calls=%fused_computation.30.clone.1 | convolution fusion | flops 1811939328 | bytes 11141632 | tf_op jit(solution)/shard_map/while/body/eval_jaxpr/kbd,kde->be/dot_general | solution.py:150
  195.5 38.8 %gather_fusion = bf16[13824,256]{1,0:T(8,128)(2,1)} fusion(bf16[2305,256]{1,0:T(8,128)(2,1)S(1)} %get-tuple-element.641, s32[14336]{0:T(1024)S(1)} %pad_clamp_fusion.4), kind=kCustom, calls=%fused_computation.clone.1 | custom fusion | bytes 14211072 | tf_op jit(solution)/shard_map/while/body/eval_jaxpr/gather | solution.py:149
  234.3 6.8 %fusion.84 = f32[4,512,256]{2,1,0:T(8,128)} fusion(f32[4,512,256]{2,1,0:T(8,128)} %get-tuple-element.633, s32[]{:T(128)} %get-tuple-element.632, bf16[27,512,256]{2,1,0:T(8,128)(2,1)} %bitcast.144, bf16[27,256,256]{2,1,0:T(8,128)(2,1)} %get-tuple-element.642), kind=kOutput, calls=%fused_computation.30.clone.1 | convolution fusion | flops 1811939328 | bytes 11141632 | tf_op jit(solution)/shard_map/while/body/eval_jaxpr/kbd,kde->be/dot_general | solution.py:150
  241.2 38.8 %gather_fusion = bf16[13824,256]{1,0:T(8,128)(2,1)} fusion(bf16[2305,256]{1,0:T(8,128)(2,1)S(1)} %get-tuple-element.641, s32[14336]{0:T(1024)S(1)} %pad_clamp_fusion.4), kind=kCustom, calls=%fused_computation.clone.1 | custom fusion | bytes 14211072 | tf_op jit(solution)/shard_map/while/body/eval_jaxpr/gather | solution.py:149
  280.0 6.8 %fusion.84 = f32[4,512,256]{2,1,0:T(8,128)} fusion(f32[4,512,256]{2,1,0:T(8,128)} %get-tuple-element.633, s32[]{:T(128)} %get-tuple-element.632, bf16[27,512,256]{2,1,0:T(8,128)(2,1)} %bitcast.144, bf16[27,256,256]{2,1,0:T(8,128)(2,1)} %get-tuple-element.642), kind=kOutput, calls=%fused_computation.30.clone.1 | convolution fusion | flops 1811939328 | bytes 11141632 | tf_op jit(solution)/shard_map/while/body/eval_jaxpr/kbd,kde->be/dot_general | solution.py:150
  286.8 2.1 add_reduce_fusion
  289.7 1.7 fusion.36
  291.4 7.4 %gather_fusion.5 = bf16[2176,256]{1,0:T(8,128)(2,1)} fusion(bf16[2048,256]{1,0:T(8,128)(2,1)S(1)} %fusion.36, s32[3072]{0:T(1024)S(1)} %pad_clamp_fusion.2), kind=kCustom, calls=%fused_computation.5 | custom fusion | bytes 2236928 | tf_op jit(solution)/shard_map/gather | solution.py:70
  298.9 2.3 broadcast_select_fusion.1
  301.2 5.1 %all-to-all-start.3 = ((bf16[8,272,256]{2,1,0:T(8,128)(2,1)}), bf16[8,272,256]{2,1,0:T(8,128)(2,1)S(1)}, u32[]{:S(2)}, u32[]{:S(2)}) async-start(bf16[8,272,256]{2,1,0:T(8,128)(2,1)} %broadcast_select_fusion.1), calls=%async_computation.3 | async-start | bytes 2228224 | tf_op jit(solution)/shard_map/all_to_all | solution.py:169
  306.9 3.1 while.78
  310.1 24.2 %all-to-all-done.3 = bf16[8,272,256]{2,1,0:T(8,128)(2,1)S(1)} async-done(((bf16[8,272,256]{2,1,0:T(8,128)(2,1)}), bf16[8,272,256]{2,1,0:T(8,128)(2,1)S(1)}, u32[]{:S(2)}, u32[]{:S(2)}) %all-to-all-start.3) | async-done | bytes 1114144 | tf_op jit(solution)/shard_map/all_to_all | solution.py:169
  334.3 3.9 %gather_fusion.6 = bf16[1024,256]{1,0:T(8,128)(2,1)S(1)} fusion(bf16[2176,256]{1,0:T(8,128)(2,1)S(1)} %bitcast.146, s32[1024]{0:T(1024)S(1)} %broadcast_clamp_fusion.1), kind=kCustom, calls=%fused_computation.6 | custom fusion | bytes 1052672 | tf_op jit(solution)/shard_map/gather | solution.py:70
  339.2 1.7 add_convert_fusion
  341.0 0.9 copy-done.16
  341.9 38.0 %while.75 = (s32[]{:T(128)}, bf16[16,1,1024,16]{2,3,1,0:T(8,128)(2,1)S(1)}, bf16[16,1,1024,16]{2,3,1,0:T(8,128)(2,1)S(1)}, bf16[16,1,1024,16]{2,3,1,0:T(8,128)(2...) while((s32[]{:T(128)}, bf16[16,1,1024,16]{2,3,1,0:T(8,128)(2,1)S(1)}, ...), condition=%wide.region_27.28_spmd, body=%wide.region_24.27_spmd.sunk | while | flops 76560384 | bytes 12736581 | solution.py:97
  343.4 0.9 fusion.87
  345.8 0.9 fusion.87
  348.2 0.9 fusion.87
  350.6 0.9 fusion.87
  357.7 0.9 fusion.87
  360.1 0.9 fusion.87
  362.4 0.9 fusion.87
  371.9 0.9 fusion.87
  374.3 0.9 fusion.87
  376.7 0.9 fusion.87
  379.9 1.2 fusion.37
  (244 shorter events, 58.0 us)
Async XLA Ops:
  0.0 21.8 %copy-start = (bf16[1024,256]{1,0:T(8,128)(2,1)S(1)}, bf16[1024,256]{1,0:T(8,128)(2,1)}, u32[]{:S(2)}) copy-start(bf16[1024,256]{1,0:T(8,128)(2,1)} %param.26) | copy-start | bytes 1572868
  15.5 35.7 %all-to-all-start.1 = ((s32[8,1,272]{2,1,0:T(1,128)}), s32[8,1,272]{2,1,0:T(1,128)S(1)}, u32[]{:S(2)}, u32[]{:S(2)}) async-start(s32[8,1,272]{2,1,0:T(1,128)} %select_n.142), calls=%async_computation.1 | async-start | bytes 24576 | tf_op jit(solution)/shard_map/all_to_all | solution.py:137
  21.8 7.2 %copy-start.6 = (s32[2048]{0:T(1024)S(1)}, s32[2048]{0:T(1024)}, u32[]{:S(2)}) copy-start(s32[2048]{0:T(1024)} %param.29) | copy-start | bytes 24580
  51.3 33.1 %all-to-all-start.2 = ((bf16[8,272,256]{2,1,0:T(8,128)(2,1)}), bf16[8,272,256]{2,1,0:T(8,128)(2,1)S(1)}, u32[]{:S(2)}, u32[]{:S(2)}) async-start(bf16[8,272,256]{2,1,0:T(8,128)(2,1)} %broadcast_select_fusion), calls=%async_computation.2 | async-start | bytes 2228224 | tf_op jit(solution)/shard_map/all_to_all | solution.py:130
  56.4 0.6 copy-start.5
  91.8 10.3 %copy-start.3 = (s32[27,2048]{1,0:T(8,128)S(1)}, s32[27,2048]{1,0:T(8,128)}, u32[]{:S(2)}) copy-start(s32[27,2048]{1,0:T(8,128)} %param.28) | copy-start | bytes 663556
  92.3 1.0 copy-start.2
  93.3 9.1 %collective-permute-start = (bf16[128,256]{1,0:T(8,128)(2,1)S(1)}, bf16[128,256]{1,0:T(8,128)(2,1)S(1)}, u32[]{:S(2)}, u32[]{:S(2)}) collective-permute-start(bf16[128,256]{1,0:T(8,128)(2,1)S(1)} %get-tuple-element.331), channel_id=1, source_target_pairs={{0,1},{1,2},{2,3},{3,4},{4,5},{5,6},{6,7},{8,9},{9,10},{10,11},{11... | collective-permute-start | bytes 196616 | tf_op jit(solution)/shard_map/ppermute | solution.py:24
  94.9 7.6 %collective-permute-start.1 = (bf16[128,256]{1,0:T(8,128)(2,1)S(1)}, bf16[128,256]{1,0:T(8,128)(2,1)S(1)}, u32[]{:S(2)}, u32[]{:S(2)}) collective-permute-start(bf16[128,256]{1,0:T(8,128)(2,1)S(1)} %get-tuple-element.332), channel_id=1, source_target_pairs={{1,0},{2,1},{3,2},{4,3},{5,4},{6,5},{7,6},{9,8},{10,9},{11,10},{12... | collective-permute-start | bytes 196616 | tf_op jit(solution)/shard_map/ppermute | solution.py:25
  96.9 204.3 %all-to-all-start = ((s32[8,1,272]{2,1,0:T(1,128)}), s32[8,1,272]{2,1,0:T(1,128)S(1)}, u32[]{:S(2)}, u32[]{:S(2)}) async-start(s32[8,1,272]{2,1,0:T(1,128)} %select_n.137), calls=%async_computation | async-start | bytes 24576 | tf_op jit(solution)/shard_map/all_to_all | solution.py:170
  104.0 182.8 %copy-start.7 = (f32[256]{0:T(256)S(1)}, f32[256]{0:T(256)}, u32[]{:S(2)}) copy-start(f32[256]{0:T(256)} %param.31) | copy-start | bytes 3076
  286.8 2.2 copy-start.1
  286.8 2.9 copy-start.8
  286.8 2.9 copy-start.9
  301.2 33.1 %all-to-all-start.3 = ((bf16[8,272,256]{2,1,0:T(8,128)(2,1)}), bf16[8,272,256]{2,1,0:T(8,128)(2,1)S(1)}, u32[]{:S(2)}, u32[]{:S(2)}) async-start(bf16[8,272,256]{2,1,0:T(8,128)(2,1)} %broadcast_select_fusion.1), calls=%async_computation.3 | async-start | bytes 2228224 | tf_op jit(solution)/shard_map/all_to_all | solution.py:169
  306.3 0.6 copy-start.4
  334.3 4.9 %copy-start.10 = (bf16[256,768]{1,0:T(8,128)(2,1)S(1)}, bf16[256,768]{1,0:T(8,128)(2,1)}, u32[]{:S(2)}) copy-start(bf16[256,768]{1,0:T(8,128)(2,1)} %param.36) | copy-start | bytes 1179652
  334.3 4.9 %copy-start.12 = (f32[768]{0:T(1024)S(1)}, f32[768]{0:T(1024)}, u32[]{:S(2)}) copy-start(f32[768]{0:T(1024)} %param.37) | copy-start | bytes 9220
  334.3 4.9 %copy-start.13 = (f32[256]{0:T(256)S(1)}, f32[256]{0:T(256)}, u32[]{:S(2)}) copy-start(f32[256]{0:T(256)} %param.35) | copy-start | bytes 3076
  334.3 4.9 %copy-start.14 = (f32[256]{0:T(256)S(1)}, f32[256]{0:T(256)}, u32[]{:S(2)}) copy-start(f32[256]{0:T(256)} %param.34) | copy-start | bytes 3076
  340.9 1.0 copy-start.16
  341.9 38.0 %copy-start.11 = (bf16[256,256]{1,0:T(8,128)(2,1)S(1)}, bf16[256,256]{1,0:T(8,128)(2,1)}, u32[]{:S(2)}) copy-start(bf16[256,256]{1,0:T(8,128)(2,1)} %param.38) | copy-start | bytes 393220
  341.9 38.0 %copy-start.15 = (f32[256]{0:T(256)S(1)}, f32[256]{0:T(256)}, u32[]{:S(2)}) copy-start(f32[256]{0:T(256)} %param.39) | copy-start | bytes 3076
where the time goes:
time: 382 us; the launch traced here: 381 us
  local copies, waits for them, and re-layouts  208 us (54%)
  matrix products  58.2 us (15%)
  waiting for transfers between devices  45.3 us (12%)
  other arithmetic  43.8 us (11%)
  starting transfers between devices  24.6 us (6%)
    gather x4, local copies, waits for them, and re-layouts, conv_block(): pulled = extended[lookup]  155 us
    dot_general x4, matrix products, conv_block(): jnp.einsum('kbd,kde->be', pulled, conv_weight, preferred_element_type=jnp...  27.3 us
    gather x4, local copies, waits for them, and re-layouts, pick_rows(): return jnp.where(found[:, None], rows[source], jnp.zeros((), rows.dtype))  25.9 us
    all_to_all x1, waiting for transfers between devices, body(): lax.all_to_all(shaped[0], 'pts', split_axis=0, concat_axis=0, tiled=True)  24.2 us
    all_to_all x1, waiting for transfers between devices, body(): lax.all_to_all(out_rows.reshape(num_peers, send_cap, model_width), 'pts',...  21.1 us
    dot_general x16, matrix products, one_head(): jnp.einsum('pqk,pkd->pqd', weights, value_h, preferred_element_type=jnp.f...  14 us
    dot_general x16, matrix products, one_head(): jnp.einsum('pqd,pkd->pqk', query_h, key_h, preferred_element_type=jnp.flo...  12.1 us
    reduce_sum x16, other arithmetic, one_head(): row_sum = jnp.sum(lifted, axis=-1, keepdims=True)  11.7 us
  transfers between devices with their start and end apart: 6, of which 2 were waited for; matrix products, arithmetic and copies ran while one was open for 62% of the time, Pallas kernels for 0%

commit v1 on v0

v1 whole, which is shorter than its diff:
```python
import functools

import jax
import jax.numpy as jnp
from jax import lax
from jax.experimental import pallas as pl
from jax.experimental.pallas import tpu as pltpu
from jax.sharding import PartitionSpec as P

HEADS = 16
HD = 16
PATCH = 1024
PTS_DEV = 1024
OWN_CAP = 2048
HALO = 128
OFFSETS = 27
CENTRE = 13
CONV_BLOCK = 544
LANES = 128
QUERY_BLOCK = 256


EPSILON = 1e-05


def layer_norm(values, gain_vec, shift_vec):
    average = jnp.mean(values, axis=-1, keepdims=True)
    centred = values - average
    spread = jnp.mean(centred * centred, axis=-1, keepdims=True)
    return centred * lax.rsqrt(spread + EPSILON) * gain_vec + shift_vec


def arrival_rank(targets, wanted, num_peers):
    row_count = targets.shape[0]
    onehot = jnp.logical_and(targets[:, None] == jnp.arange(num_peers)[None, :], wanted[:, None])
    onehot_bf = onehot.astype(jnp.bfloat16)
    line = jnp.arange(row_count)
    lower = (line[None, :] < line[:, None]).astype(jnp.bfloat16)
    earlier = jnp.dot(lower, onehot_bf, preferred_element_type=jnp.float32)
    return jnp.sum(earlier * onehot.astype(jnp.float32), axis=1).astype(jnp.int32)


def buffer_index(targets, wanted, num_peers, stride, overflow):
    ranking = arrival_rank(targets, wanted, num_peers)
    return jnp.where(wanted, targets * stride + ranking, overflow)


def place_matrix(where_to, count):
    return (jnp.arange(count)[:, None] == where_to[None, :]).astype(jnp.bfloat16)


def place_rows(where_to, rows, count):
    return jnp.dot(
        place_matrix(where_to, count), rows, preferred_element_type=jnp.float32
    ).astype(jnp.bfloat16)


def place_numbers(where_to, numbers, missing, count):
    match = jnp.arange(count)[:, None] == where_to[None, :]
    return missing + jnp.sum(jnp.where(match, numbers[None, :] - missing, 0), axis=1)


def swap(values, num_peers):
    return lax.all_to_all(
        values.reshape((num_peers, -1) + values.shape[1:]),
        "pts",
        split_axis=0,
        concat_axis=0,
        tiled=True,
    ).reshape(values.shape)


def conv_kernel(
    block, table_ref, ext_ref, weight_ref, bias_ref, gain_ref, shift_ref,
    out_ref, rows_ref, pulled_ref, acc_ref,
):
    held = ext_ref.shape[0]

    @pl.when(pl.program_id(0) == 0)
    def _():
        chunk = 256

        def put(step, carry):
            base = pl.multiple_of(step * chunk, chunk)
            part = ext_ref[pl.ds(base, chunk), :].astype(jnp.float32)
            rows_ref[pl.ds(2 * base, chunk, stride=2), :] = part[:, :LANES]
            rows_ref[pl.ds(2 * base + 1, chunk, stride=2), :] = part[:, LANES:]
            return carry

        lax.fori_loop(0, held // chunk, put, 0)
        rows_ref[pl.ds(2 * held, 8), :] = jnp.zeros((8, LANES), jnp.float32)

    acc_ref[...] = jnp.zeros_like(acc_ref)

    def pull(offset):
        for row in range(block):
            at = pl.multiple_of(table_ref[0, 0, offset * block + row], 2)
            pulled_ref[pl.ds(2 * row, 2), :] = rows_ref[pl.ds(at, 2), :]

    def pulled_rows():
        return jnp.concatenate(
            [pulled_ref[pl.ds(0, block, stride=2), :], pulled_ref[pl.ds(1, block, stride=2), :]],
            axis=1,
        )

    def multiply(which):
        acc_ref[...] += jnp.dot(
            pulled_rows().astype(jnp.bfloat16),
            weight_ref[which],
            preferred_element_type=jnp.float32,
        )

    pull(0)

    def one(offset, carry):
        multiply(offset + (offset >= CENTRE).astype(jnp.int32))
        pull(offset + 1)
        return carry

    lax.fori_loop(0, OFFSETS - 1, one, 0)
    multiply(CENTRE)
    encoded = layer_norm(acc_ref[...] + bias_ref[...], gain_ref[...], shift_ref[...])
    out_ref[...] = (pulled_rows() + encoded).astype(jnp.bfloat16)


def conv_rows(table, extended, conv_weight, conv_bias, cpe_gain, cpe_bias):
    count = table.shape[1]
    block = CONV_BLOCK if count % CONV_BLOCK == 0 else count
    steps = count // block
    held, width = extended.shape
    lookup = table.reshape(OFFSETS, steps, block).transpose(1, 0, 2).reshape(
        steps, 1, OFFSETS * block
    )
    return pl.pallas_call(
        functools.partial(conv_kernel, block),
        grid=(steps,),
        out_shape=jax.ShapeDtypeStruct((count, width), jnp.bfloat16),
        in_specs=[
            pl.BlockSpec((1, 1, OFFSETS * block), lambda i: (i, 0, 0), memory_space=pltpu.SMEM)
        ]
        + [pl.BlockSpec(memory_space=pltpu.VMEM)] * 5,
        out_specs=pl.BlockSpec((block, width), lambda i: (i, 0)),
        scratch_shapes=[
            pltpu.VMEM((2 * held + 8, LANES), jnp.float32),
            pltpu.VMEM((2 * block, LANES), jnp.float32),
            pltpu.VMEM((block, width), jnp.float32),
        ],
        compiler_params=pltpu.CompilerParams(vmem_limit_bytes=32 * 2**20),
        cost_estimate=pl.CostEstimate(
            flops=2 * count * OFFSETS * width * width,
            bytes_accessed=conv_weight.size * 2 + count * width * 4,
            transcendentals=0,
        ),
    )(
        lookup, extended, conv_weight, conv_bias[None, :], cpe_gain[None, :], cpe_bias[None, :]
    )


def attend_kernel(
    got_ref, spots_ref, gain_ref, shift_ref, qkv_ref, qkv_bias_ref, proj_ref, proj_bias_ref,
    out_ref, placed_ref, heads_ref, attended_ref,
):
    rows, width = out_ref.shape
    size = QUERY_BLOCK
    for start in range(0, rows, size):
        line = lax.broadcasted_iota(jnp.int32, (size, 1), 0) + start
        match = jnp.where(spots_ref[...] == line, 1.0, 0.0).astype(jnp.bfloat16)
        placed = jnp.dot(match, got_ref[...], preferred_element_type=jnp.float32)
        placed_ref[pl.ds(start, size), :] = placed
        normed = layer_norm(placed, gain_ref[...], shift_ref[...]).astype(jnp.bfloat16)
        product = lax.dot_general(
            qkv_ref[...], normed, (((1,), (1,)), ((), ())), preferred_element_type=jnp.float32
        )
        heads_ref[:, pl.ds(start, size)] = (product + qkv_bias_ref[...]).astype(jnp.bfloat16)

    factor = HD ** (-0.5) * 1.4426950408889634

    def one_head(head, carry):
        base = pl.multiple_of(head * HD, HD)
        keys = heads_ref[pl.ds(width + base, HD), :]
        values = heads_ref[pl.ds(2 * width + base, HD), :]
        widened = jnp.concatenate([values, jnp.ones_like(values)], axis=0)
        for start in range(0, rows, size):
            queries = heads_ref[pl.ds(base, HD), pl.ds(start, size)]
            scores = lax.dot_general(
                keys, queries, (((0,), (0,)), ((), ())), preferred_element_type=jnp.float32
            )
            highest = jnp.max(scores, axis=0, keepdims=True)
            lifted = jnp.exp2((scores - highest) * factor).astype(jnp.bfloat16)
            summed = jnp.dot(widened, lifted, preferred_element_type=jnp.float32)
            attended_ref[pl.ds(base, HD), pl.ds(start, size)] = (
                summed[:HD] / summed[HD : HD + 1]
            ).astype(jnp.bfloat16)
        return carry

    lax.fori_loop(0, HEADS, one_head, 0)
    for start in range(0, rows, size):
        projected = lax.dot_general(
            attended_ref[:, pl.ds(start, size)],
            proj_ref[...],
            (((0,), (0,)), ((), ())),
            preferred_element_type=jnp.float32,
        )
        out_ref[pl.ds(start, size), :] = (
            placed_ref[pl.ds(start, size), :] + projected + proj_bias_ref[...]
        ).astype(jnp.bfloat16)


def attend_rows(
    got, spots, norm_gain, norm_bias, qkv_weight, qkv_bias, proj_weight, proj_bias, rows
):
    width = got.shape[1]
    return pl.pallas_call(
        attend_kernel,
        out_shape=jax.ShapeDtypeStruct((rows, width), jnp.bfloat16),
        in_specs=[pl.BlockSpec(memory_space=pltpu.VMEM)] * 8,
        out_specs=pl.BlockSpec(memory_space=pltpu.VMEM),
        scratch_shapes=[
            pltpu.VMEM((rows, width), jnp.float32),
            pltpu.VMEM((3 * width, rows), jnp.bfloat16),
            pltpu.VMEM((width, rows), jnp.bfloat16),
        ],
        compiler_params=pltpu.CompilerParams(vmem_limit_bytes=40 * 2**20),
    )(
        got, spots[None, :], norm_gain[None, :], norm_bias[None, :], qkv_weight.T,
        qkv_bias[:, None], proj_weight, proj_bias[None, :],
    )


def body(
    features,
    tile_slot,
    neighbors,
    serial,
    conv_weight,
    conv_bias,
    cpe_gain,
    cpe_bias,
    norm_gain,
    norm_bias,
    qkv_weight,
    qkv_bias,
    proj_weight,
    proj_bias,
):
    num_peers = lax.axis_size("pts")
    local_rows = features.shape[0]
    send_cap = 17 * local_rows // (8 * num_peers)
    total = num_peers * send_cap

    owners = tile_slot // OWN_CAP
    slot_in = tile_slot % OWN_CAP
    where_to = buffer_index(owners, jnp.ones(owners.shape, bool), num_peers, send_cap, total)
    got_slots = swap(place_numbers(where_to, slot_in, OWN_CAP, total), num_peers)
    got_rows = swap(place_rows(where_to, features, total), num_peers)
    line = jnp.arange(OWN_CAP)
    tiled_rows = jnp.dot(
        (line[:, None] == got_slots[None, :]).astype(jnp.bfloat16),
        got_rows,
        preferred_element_type=jnp.float32,
    ).astype(jnp.bfloat16)
    up = [(i, i + 1) for i in range(num_peers - 1)]
    down = [(i + 1, i) for i in range(num_peers - 1)]
    before = lax.ppermute(tiled_rows[OWN_CAP - HALO :], "pts", up)
    after = lax.ppermute(tiled_rows[:HALO], "pts", down)
    extended = jnp.concatenate([before, tiled_rows, after], axis=0)

    placed_ok = serial >= 0
    devices_to = jnp.where(placed_ok, serial // PTS_DEV, 0)
    where_to = buffer_index(devices_to, placed_ok, num_peers, send_cap, total)
    spots = place_numbers(where_to, serial % PTS_DEV, PTS_DEV, total)
    got_spots = swap(spots, num_peers)
    ordered = jnp.concatenate(
        [neighbors[:CENTRE], neighbors[CENTRE + 1 :], neighbors[CENTRE : CENTRE + 1]], axis=0
    )
    digits = jnp.concatenate([ordered // 64, ordered % 64], axis=0).astype(jnp.bfloat16)
    moved = lax.dot_general(
        digits,
        place_matrix(where_to, total),
        (((1,), (1,)), ((), ())),
        preferred_element_type=jnp.float32,
    )
    table = (moved[:OFFSETS] * 128 + moved[OFFSETS:] * 2).astype(jnp.int32)
    hidden = conv_rows(table, extended, conv_weight, conv_bias, cpe_gain, cpe_bias)
    got = swap(hidden, num_peers)
    return attend_rows(
        got, got_spots, norm_gain, norm_bias, qkv_weight, qkv_bias, proj_weight, proj_bias,
        local_rows,
    )


def solution(mesh):
    placed = (
        P(("dp", "pts"), None),
        P(("dp", "pts")),
        P(None, ("dp", "pts")),
        P(("dp", "pts")),
        P(),
        P(),
        P(),
        P(),
        P(),
        P(),
        P(),
        P(),
        P(),
        P(),
    )
    return jax.shard_map(
        body, mesh=mesh, in_specs=placed, out_specs=P(("dp", "pts"), None), check_vma=False
    )
```

time: 382 us -> 204 us (0.53)
  local copies, waits for them, and re-layouts: 208 us -> 4.59 us
  Pallas kernels: 0 us -> 106 us
  matrix products: 58.2 us -> 11.3 us
  other arithmetic: 43.8 us -> 4.82 us
  waiting for transfers between devices: 45.3 us -> 52.8 us
    gather x10 -> x0, local copies, waits for them, and re-layouts: 201 us -> none  [the longest x4 155 us: conv_block(): pulled = extended[lookup]]
    pallas_call x0 -> x2, Pallas kernels: none -> 106 us  [the longest x1 54.2 us: conv_rows(): pl.pallas_call(functools.partial(conv_kernel, block), grid=(steps,), out_...]
    dot_general x38 -> x3, matrix products: 56.3 us -> 9.45 us  [the longest x1 3.41 us: body(): lax.dot_general(digits, place_matrix(where_to, total), (((1,), (1,)), (()...]
    reduce_sum x36 -> x2, other arithmetic: 25.4 us -> 2.83 us  [place_numbers(): jnp.sum(jnp.where(match, numbers[None, :] - missing, 0), axis=1)]
    reduce_or x16 -> x0, other arithmetic: 9.3 us -> none  [one_block(): return (source, jnp.any(match, axis=1))]
    all_to_all x4, waiting for transfers between devices: 45.3 us -> 50.5 us  [swap(): lax.all_to_all(values.reshape((num_peers, -1) + values.shape[1:]), 'pts',...]
    select_n x15 -> x0, other arithmetic: 4.9 us -> none  [the longest x5 4.12 us: pick_rows(): return jnp.where(found[:, None], rows[source], jnp.zeros((), rows.dtype))]
  transfers between devices with their start and end apart: 6 -> 6, of which waited for: 2 -> 4; matrix products, arithmetic and copies ran while one was open for 62% -> 7% of each run, Pallas kernels for 0% -> 27%
where the time goes in v1:
time: 204 us; the launch traced here: 203 us
  Pallas kernels  106 us (52%)
  waiting for transfers between devices  52.8 us (26%)
  starting transfers between devices  23.4 us (11%)
  matrix products  11.3 us (6%)
  other arithmetic  4.82 us (2%)
  local copies, waits for them, and re-layouts  4.59 us (2%)
    pallas_call x1, Pallas kernels, conv_rows(): pl.pallas_call(functools.partial(conv_kernel, block), grid=(steps,), out_...  54.2 us
    pallas_call x1, Pallas kernels, attend_rows(): pl.pallas_call(attend_kernel, out_shape=jax.ShapeDtypeStruct((rows, width...  51.6 us
    all_to_all x4, waiting for transfers between devices, swap(): lax.all_to_all(values.reshape((num_peers, -1) + values.shape[1:]), 'pts',...  50.5 us
    all_to_all x4, starting transfers between devices, swap(): lax.all_to_all(values.reshape((num_peers, -1) + values.shape[1:]), 'pts',...  20 us
  transfers between devices with their start and end apart: 6, of which 4 were waited for; matrix products, arithmetic and copies ran while one was open for 7% of the time, Pallas kernels for 27%

profile of v1, /device:TPU:0, one launch (start us, length us, event | category | flops | bytes accessed | tf_op | source)
XLA Modules:
  0.0 203.0 jit_solution(10721297760037623317)
XLA Ops:
  0.0 0.0 copy-start
  0.0 0.8 add_select_fusion.6
  0.8 0.5 fusion.13
  1.2 0.7 fusion.31
  1.9 1.0 select_reduce_fusion.1
  2.9 0.7 add.75
  3.6 6.3 %all-to-all-start = ((s32[8,1,272]{2,1,0:T(1,128)}), s32[8,1,272]{2,1,0:T(1,128)S(1)}, u32[]{:S(2)}, u32[]{:S(2)}) async-start(s32[8,1,272]{2,1,0:T(1,128)} %add.75), calls=%async_computation | async-start | bytes 24576 | tf_op jit(solution)/shard_map/all_to_all | solution.py:64
  10.0 0.0 copy-done
  10.0 0.0 copy-start.11
  10.0 2.7 %fusion.8 = bf16[2176,256]{1,0:T(8,128)(2,1)} fusion(bf16[1024,256]{1,0:T(8,128)(2,1)S(1)} %copy-done, s32[1024]{0:T(1024)S(1)} %get-tuple-element.16), kind=kOutput, calls=%fused_computation.15 | convolution fusion | flops 1143635968 | bytes 1642496 | tf_op jit(solution)/shard_map/dot_general | solution.py:53
  12.7 1.4 fusion.11
  14.2 1.4 all-to-all-done
  15.6 3.7 %all-to-all-start.1 = ((bf16[8,272,256]{2,1,0:T(8,128)(2,1)}), bf16[8,272,256]{2,1,0:T(8,128)(2,1)S(1)}, u32[]{:S(2)}, u32[]{:S(2)}) async-start(bf16[8,272,256]{2,1,0:T(8,128)(2,1)} %bitcast.1), calls=%async_computation.1 | async-start | bytes 2228224 | tf_op jit(solution)/shard_map/all_to_all | solution.py:64
  19.3 1.9 select_reduce_fusion
  21.2 0.7 add.79
  21.9 0.3 fusion.16
  22.2 3.4 %fusion = f32[54,2176]{1,0:T(8,128)S(1)} fusion(s32[2048]{0:T(1024)S(1)} %get-tuple-element.14, bf16[27,2048]{1,0:T(8,128)(2,1)S(1)} %get-tuple-element.10, bf16[27,2048]{1,0:T(8,128)(2,1)S(1)} %get-tuple-element.9), kind=kOutput, calls=%fused_computation.3 | convolution fusion | flops 486195200 | bytes 699392 | tf_op jit(solution)/shard_map/dot_general | solution.py:277
  25.6 0.1 eq.51
  25.7 21.6 %all-to-all-done.1 = bf16[8,272,256]{2,1,0:T(8,128)(2,1)S(1)} async-done(((bf16[8,272,256]{2,1,0:T(8,128)(2,1)}), bf16[8,272,256]{2,1,0:T(8,128)(2,1)S(1)}, u32[]{:S(2)}, u32[]{:S(2)}) %all-to-all-start.1) | async-done | bytes 1114144 | tf_op jit(solution)/shard_map/all_to_all | solution.py:64
  47.3 3.5 %all-to-all-start.3 = ((s32[8,1,272]{2,1,0:T(1,128)}), s32[8,1,272]{2,1,0:T(1,128)S(1)}, u32[]{:S(2)}, u32[]{:S(2)}) async-start(s32[8,1,272]{2,1,0:T(1,128)} %add.79), calls=%async_computation.3 | async-start | bytes 24576 | tf_op jit(solution)/shard_map/all_to_all | solution.py:64
  50.8 3.3 %fusion.9 = bf16[2048,256]{1,0:T(8,128)(2,1)S(1)} fusion(bf16[2176,256]{1,0:T(8,128)(2,1)S(1)} %bitcast.25, s32[2176]{0:T(1024)S(1)} %eq.51), kind=kOutput, calls=%fused_computation.16 | convolution fusion | flops 2286682112 | bytes 2171392 | tf_op jit(solution)/shard_map/dot_general | solution.py:257
  54.1 0.0 copy-start.6
  54.1 0.0 copy-start.7
  54.1 0.0 copy-start.8
  54.2 2.1 %collective-permute-start = (bf16[128,256]{1,0:T(8,128)(2,1)S(1)}, bf16[128,256]{1,0:T(8,128)(2,1)S(1)}, u32[]{:S(2)}, u32[]{:S(2)}) collective-permute-start(bf16[128,256]{1,0:T(8,128)(2,1)S(1)} %get-tuple-element.7), channel_id=1, source_target_pairs={{0,1},{1,2},{2,3},{3,4},{4,5},{5,6},{6,7},{8,9},{9,10},{10,11},{11... | collective-permute-start | bytes 196616 | tf_op jit(solution)/shard_map/ppermute | solution.py:264
  56.3 1.3 collective-permute-start.1
  57.6 0.1 fusion.15
  57.7 0.2 reshape.62
  57.9 0.4 reshape.68.table_ref
  58.3 0.0 collective-permute-done
  58.3 2.3 %collective-permute-done.1 = bf16[128,256]{1,0:T(8,128)(2,1)S(1)} collective-permute-done((bf16[128,256]{1,0:T(8,128)(2,1)S(1)}, bf16[128,256]{1,0:T(8,128)(2,1)S(1)}, u32[]{:S(2)}, u32[]{:S(2)}) %collective-permute-start.1) | collective-permute-done | bytes 65568 | tf_op jit(solution)/shard_map/ppermute | solution.py:265
  60.6 0.1 pad_maximum_fusion.ext_ref
  60.7 0.0 copy-done.6
  60.7 0.0 copy-done.7
  60.7 0.0 copy-done.8
  60.7 0.0 copy-start.5
  60.7 2.0 copy-done.5
  62.7 0.0 copy-start.4
  62.7 54.2 %shard_map.136 = bf16[2176,256]{1,0:T(8,128)(2,1)} custom-call(s32[4,1,14688]{2,1,0:T(1,128)S(1)} %reshape.68.table_ref, bf16[2304,256]{1,0:T(8,128)(2,1)S(1)} %pad_maximum_fusion.ext_ref, bf16[27,256,256]{2,1,0:T(8,128)(2,1)S(1)} %copy-done.5, f32[1,256]{1,0:T(1,128)S(1)} %bitcast.21, f32[1,256]{1,0:T(1,128)S(1)} %bitcast.22, f32[1,256]{1,0:T(1,128)S(1)} %bitcast.23), custom_call_target="tpu_custom_call" | custom-call | flops 7700742144 | bytes 5767168 | tf_op jit(solution)/shard_map/pallas_call | solution.py:134
  117.0 0.0 all-to-all-done.3
  117.0 6.4 %all-to-all-start.2 = ((bf16[8,272,256]{2,1,0:T(8,128)(2,1)}), bf16[8,272,256]{2,1,0:T(8,128)(2,1)S(1)}, u32[]{:S(2)}, u32[]{:S(2)}) async-start(bf16[8,272,256]{2,1,0:T(8,128)(2,1)} %bitcast.6), calls=%async_computation.2 | async-start | bytes 2228224 | tf_op jit(solution)/shard_map/all_to_all | solution.py:64
  123.4 0.2 copy.27
  123.6 0.0 copy-done.12
  123.6 0.2 broadcast_in_dim.85.qkv_bias_ref
  123.8 0.1 broadcast_in_dim_reshape.4.spots_ref
  123.9 27.5 %all-to-all-done.2 = bf16[8,272,256]{2,1,0:T(8,128)(2,1)S(1)} async-done(((bf16[8,272,256]{2,1,0:T(8,128)(2,1)}), bf16[8,272,256]{2,1,0:T(8,128)(2,1)S(1)}, u32[]{:S(2)}, u32[]{:S(2)}) %all-to-all-start.2) | async-done | bytes 1114144 | tf_op jit(solution)/shard_map/all_to_all | solution.py:64
  151.4 0.0 copy-done.4
  151.4 51.6 %shard_map.137 = bf16[1024,256]{1,0:T(8,128)(2,1)} custom-call(bf16[2176,256]{1,0:T(8,128)(2,1)S(1)} %bitcast.16, s32[1,2176]{1,0:T(1,128)S(1)} %broadcast_in_dim_reshape.4.spots_ref, f32[1,256]{1,0:T(1,128)S(1)} %bitcast.18, f32[1,256]{1,0:T(1,128)S(1)} %bitcast.19, bf16[768,256]{1,0:T(8,128)(2,1)S(1)} %bitcast.17, ...), custom_call_target="tpu_custom_call" | custom-call | tf_op jit(solution)/shard_map/pallas_call | solution.py:213
  (22 shorter events, 0.2 us)
Async XLA Ops:
  0.0 10.0 %copy-start = (bf16[1024,256]{1,0:T(8,128)(2,1)S(1)}, bf16[1024,256]{1,0:T(8,128)(2,1)}, u32[]{:S(2)}) copy-start(bf16[1024,256]{1,0:T(8,128)(2,1)} %param.14) | copy-start | bytes 1572868
  3.6 12.0 %all-to-all-start = ((s32[8,1,272]{2,1,0:T(1,128)}), s32[8,1,272]{2,1,0:T(1,128)S(1)}, u32[]{:S(2)}, u32[]{:S(2)}) async-start(s32[8,1,272]{2,1,0:T(1,128)} %add.75), calls=%async_computation | async-start | bytes 24576 | tf_op jit(solution)/shard_map/all_to_all | solution.py:64
  10.0 2.7 %copy-start.11 = (s32[2048]{0:T(1024)S(1)}, s32[2048]{0:T(1024)}, u32[]{:S(2)}) copy-start(s32[2048]{0:T(1024)} %param.17) | copy-start | bytes 24580
  12.7 1.5 copy-start.10
  15.6 31.7 %all-to-all-start.1 = ((bf16[8,272,256]{2,1,0:T(8,128)(2,1)}), bf16[8,272,256]{2,1,0:T(8,128)(2,1)S(1)}, u32[]{:S(2)}, u32[]{:S(2)}) async-start(bf16[8,272,256]{2,1,0:T(8,128)(2,1)} %bitcast.1), calls=%async_computation.1 | async-start | bytes 2228224 | tf_op jit(solution)/shard_map/all_to_all | solution.py:64
  47.3 69.7 %all-to-all-start.3 = ((s32[8,1,272]{2,1,0:T(1,128)}), s32[8,1,272]{2,1,0:T(1,128)S(1)}, u32[]{:S(2)}, u32[]{:S(2)}) async-start(s32[8,1,272]{2,1,0:T(1,128)} %add.79), calls=%async_computation.3 | async-start | bytes 24576 | tf_op jit(solution)/shard_map/all_to_all | solution.py:64
  54.1 6.6 %copy-start.6 = (f32[256]{0:T(256)S(1)}, f32[256]{0:T(256)}, u32[]{:S(2)}) copy-start(f32[256]{0:T(256)} %param.19) | copy-start | bytes 3076
  54.1 6.6 %copy-start.7 = (f32[256]{0:T(256)S(1)}, f32[256]{0:T(256)}, u32[]{:S(2)}) copy-start(f32[256]{0:T(256)} %param.20) | copy-start | bytes 3076
  54.1 6.6 %copy-start.8 = (f32[256]{0:T(256)S(1)}, f32[256]{0:T(256)}, u32[]{:S(2)}) copy-start(f32[256]{0:T(256)} %param.21) | copy-start | bytes 3076
  54.2 4.1 %collective-permute-start = (bf16[128,256]{1,0:T(8,128)(2,1)S(1)}, bf16[128,256]{1,0:T(8,128)(2,1)S(1)}, u32[]{:S(2)}, u32[]{:S(2)}) collective-permute-start(bf16[128,256]{1,0:T(8,128)(2,1)S(1)} %get-tuple-element.7), channel_id=1, source_target_pairs={{0,1},{1,2},{2,3},{3,4},{4,5},{5,6},{6,7},{8,9},{9,10},{10,11},{11... | collective-permute-start | bytes 196616 | tf_op jit(solution)/shard_map/ppermute | solution.py:264
  56.3 4.3 %collective-permute-start.1 = (bf16[128,256]{1,0:T(8,128)(2,1)S(1)}, bf16[128,256]{1,0:T(8,128)(2,1)S(1)}, u32[]{:S(2)}, u32[]{:S(2)}) collective-permute-start(bf16[128,256]{1,0:T(8,128)(2,1)S(1)} %get-tuple-element.8), channel_id=1, source_target_pairs={{1,0},{2,1},{3,2},{4,3},{5,4},{6,5},{7,6},{9,8},{10,9},{11,10},{12... | collective-permute-start | bytes 196616 | tf_op jit(solution)/shard_map/ppermute | solution.py:265
  60.7 2.0 copy-start.5
  62.7 60.7 %copy-start.9 = (bf16[256,768]{1,0:T(8,128)(2,1)S(1)}, bf16[256,768]{1,0:T(8,128)(2,1)}, u32[]{:S(2)}) copy-start(bf16[256,768]{1,0:T(8,128)(2,1)} %param.24) | copy-start | bytes 1179652
  62.7 60.9 %copy-start.12 = (f32[768]{0:T(1024)S(1)}, f32[768]{0:T(1024)}, u32[]{:S(2)}) copy-start(f32[768]{0:T(1024)} %param.25) | copy-start | bytes 9220
  62.7 88.7 %copy-start.2 = (f32[256]{0:T(256)S(1)}, f32[256]{0:T(256)}, u32[]{:S(2)}) copy-start(f32[256]{0:T(256)} %param.22) | copy-start | bytes 3076
  62.7 88.7 %copy-start.3 = (f32[256]{0:T(256)S(1)}, f32[256]{0:T(256)}, u32[]{:S(2)}) copy-start(f32[256]{0:T(256)} %param.23) | copy-start | bytes 3076
  62.7 88.7 %copy-start.4 = (f32[256]{0:T(256)S(1)}, f32[256]{0:T(256)}, u32[]{:S(2)}) copy-start(f32[256]{0:T(256)} %param.27) | copy-start | bytes 3076
  117.0 34.5 %copy-start.1 = (bf16[256,256]{1,0:T(8,128)(2,1)S(1)}, bf16[256,256]{1,0:T(8,128)(2,1)}, u32[]{:S(2)}) copy-start(bf16[256,256]{1,0:T(8,128)(2,1)} %proj_ref.1) | copy-start | bytes 393220
  117.0 34.4 %all-to-all-start.2 = ((bf16[8,272,256]{2,1,0:T(8,128)(2,1)}), bf16[8,272,256]{2,1,0:T(8,128)(2,1)S(1)}, u32[]{:S(2)}, u32[]{:S(2)}) async-start(bf16[8,272,256]{2,1,0:T(8,128)(2,1)} %bitcast.6), calls=%async_computation.2 | async-start | bytes 2228224 | tf_op jit(solution)/shard_map/all_to_all | solution.py:64

commit v2 on v1

--- a/solution.py
+++ b/solution.py
@@ -15,9 +15,10 @@
 HALO = 128
 OFFSETS = 27
 CENTRE = 13
-CONV_BLOCK = 544
+CONV_BLOCK = 768
+FIRST_SHARE = (22, 34)
 LANES = 128
-QUERY_BLOCK = 256
+ROW_BLOCK = 256
 
 
 EPSILON = 1e-05
@@ -125,8 +126,8 @@
 
 def conv_rows(table, extended, conv_weight, conv_bias, cpe_gain, cpe_bias):
     count = table.shape[1]
-    block = CONV_BLOCK if count % CONV_BLOCK == 0 else count
-    steps = count // block
+    steps = -(-count // CONV_BLOCK)
+    block = count // steps
     held, width = extended.shape
     lookup = table.reshape(OFFSETS, steps, block).transpose(1, 0, 2).reshape(
         steps, 1, OFFSETS * block
@@ -157,15 +158,17 @@
 
 
 def attend_kernel(
-    got_ref, spots_ref, gain_ref, shift_ref, qkv_ref, qkv_bias_ref, proj_ref, proj_bias_ref,
-    out_ref, placed_ref, heads_ref, attended_ref,
+    first_ref, last_ref, first_spots_ref, last_spots_ref, gain_ref, shift_ref, qkv_ref, qkv_bias_ref,
+    proj_ref, proj_bias_ref, out_ref, placed_ref, heads_ref, attended_ref,
 ):
     rows, width = out_ref.shape
-    size = QUERY_BLOCK
+    size = ROW_BLOCK
     for start in range(0, rows, size):
         line = lax.broadcasted_iota(jnp.int32, (size, 1), 0) + start
-        match = jnp.where(spots_ref[...] == line, 1.0, 0.0).astype(jnp.bfloat16)
-        placed = jnp.dot(match, got_ref[...], preferred_element_type=jnp.float32)
+        placed = 0.0
+        for got_ref, spots_ref in ((first_ref, first_spots_ref), (last_ref, last_spots_ref)):
+            match = jnp.where(spots_ref[...] == line, 1.0, 0.0).astype(jnp.bfloat16)
+            placed += jnp.dot(match, got_ref[...], preferred_element_type=jnp.float32)
         placed_ref[pl.ds(start, size), :] = placed
         normed = layer_norm(placed, gain_ref[...], shift_ref[...]).astype(jnp.bfloat16)
         product = lax.dot_general(
@@ -180,20 +183,15 @@
         keys = heads_ref[pl.ds(width + base, HD), :]
         values = heads_ref[pl.ds(2 * width + base, HD), :]
         widened = jnp.concatenate([values, jnp.ones_like(values)], axis=0)
-        for start in range(0, rows, size):
-            queries = heads_ref[pl.ds(base, HD), pl.ds(start, size)]
-            scores = lax.dot_general(
-                keys, queries, (((0,), (0,)), ((), ())), preferred_element_type=jnp.float32
-            )
-            highest = jnp.max(scores, axis=0, keepdims=True)
-            lifted = jnp.exp2((scores - highest) * factor).astype(jnp.bfloat16)
-            summed = jnp.dot(widened, lifted, preferred_element_type=jnp.float32)
-            attended_ref[pl.ds(base, HD), pl.ds(start, size)] = (
-                summed[:HD] / summed[HD : HD + 1]
-            ).astype(jnp.bfloat16)
+        queries = heads_ref[pl.ds(base, HD), :]
+        scores = jnp.dot(keys.T, queries, preferred_element_type=jnp.float32)
+        highest = jnp.max(scores, axis=0, keepdims=True)
+        lifted = jnp.exp2((scores - highest) * factor).astype(jnp.bfloat16)
+        summed = jnp.dot(widened, lifted, preferred_element_type=jnp.float32)
+        attended_ref[pl.ds(base, HD), :] = (summed[:HD] / summed[HD : HD + 1]).astype(jnp.bfloat16)
         return carry
 
-    lax.fori_loop(0, HEADS, one_head, 0)
+    lax.fori_loop(0, HEADS, one_head, 0, unroll=4)
     for start in range(0, rows, size):
         projected = lax.dot_general(
             attended_ref[:, pl.ds(start, size)],
@@ -207,22 +205,23 @@
 
 
 def attend_rows(
-    got, spots, norm_gain, norm_bias, qkv_weight, qkv_bias, proj_weight, proj_bias, rows
+    first, last, first_spots, last_spots, norm_gain, norm_bias, qkv_weight, qkv_bias,
+    proj_weight, proj_bias, rows,
 ):
-    width = got.shape[1]
+    width = first.shape[1]
     return pl.pallas_call(
         attend_kernel,
         out_shape=jax.ShapeDtypeStruct((rows, width), jnp.bfloat16),
-        in_specs=[pl.BlockSpec(memory_space=pltpu.VMEM)] * 8,
+        in_specs=[pl.BlockSpec(memory_space=pltpu.VMEM)] * 10,
         out_specs=pl.BlockSpec(memory_space=pltpu.VMEM),
         scratch_shapes=[
             pltpu.VMEM((rows, width), jnp.float32),
             pltpu.VMEM((3 * width, rows), jnp.bfloat16),
             pltpu.VMEM((width, rows), jnp.bfloat16),
         ],
-        compiler_params=pltpu.CompilerParams(vmem_limit_bytes=40 * 2**20),
+        compiler_params=pltpu.CompilerParams(vmem_limit_bytes=50 * 2**20),
     )(
-        got, spots[None, :], norm_gain[None, :], norm_bias[None, :], qkv_weight.T,
+        first, last, first_spots[None, :], last_spots[None, :], norm_gain[None, :], norm_bias[None, :], qkv_weight.T,
         qkv_bias[:, None], proj_weight, proj_bias[None, :],
     )
 
@@ -249,43 +248,73 @@
     total = num_peers * send_cap
 
     owners = tile_slot // OWN_CAP
-    slot_in = tile_slot % OWN_CAP
     where_to = buffer_index(owners, jnp.ones(owners.shape, bool), num_peers, send_cap, total)
-    got_slots = swap(place_numbers(where_to, slot_in, OWN_CAP, total), num_peers)
-    got_rows = swap(place_rows(where_to, features, total), num_peers)
-    line = jnp.arange(OWN_CAP)
-    tiled_rows = jnp.dot(
-        (line[:, None] == got_slots[None, :]).astype(jnp.bfloat16),
-        got_rows,
-        preferred_element_type=jnp.float32,
-    ).astype(jnp.bfloat16)
-    up = [(i, i + 1) for i in range(num_peers - 1)]
-    down = [(i + 1, i) for i in range(num_peers - 1)]
-    before = lax.ppermute(tiled_rows[OWN_CAP - HALO :], "pts", up)
-    after = lax.ppermute(tiled_rows[:HALO], "pts", down)
-    extended = jnp.concatenate([before, tiled_rows, after], axis=0)
-
+    packed, serial, where_in = lax.optimization_barrier(
+        (place_rows(where_to, features, total), serial, where_to)
+    )
+    got_rows = swap(packed, num_peers)
+    slots = place_numbers(where_in, tile_slot % OWN_CAP, OWN_CAP, total)
+
+    cap_first = send_cap * FIRST_SHARE[0] // FIRST_SHARE[1]
+    cap_last = send_cap - cap_first
+    count_first = num_peers * cap_first
     placed_ok = serial >= 0
     devices_to = jnp.where(placed_ok, serial // PTS_DEV, 0)
-    where_to = buffer_index(devices_to, placed_ok, num_peers, send_cap, total)
+    ranking = arrival_rank(devices_to, placed_ok, num_peers)
+    where_to = jnp.where(placed_ok, devices_to * send_cap + ranking, total)
     spots = place_numbers(where_to, serial % PTS_DEV, PTS_DEV, total)
-    got_spots = swap(spots, num_peers)
+    numbers = lax.all_to_all(
+        jnp.concatenate(
+            [slots.reshape(num_peers, send_cap), spots.reshape(num_peers, send_cap)], axis=1
+        ),
+        "pts",
+        split_axis=0,
+        concat_axis=0,
+        tiled=True,
+    )
+    got_slots = numbers[:, :send_cap].reshape(-1)
+    first_spots = numbers[:, send_cap : send_cap + cap_first].reshape(-1)
+    last_spots = numbers[:, send_cap + cap_first :].reshape(-1)
+
+    order = jnp.where(
+        ranking < cap_first,
+        devices_to * cap_first + ranking,
+        count_first + devices_to * cap_last + ranking - cap_first,
+    )
+    order = jnp.where(placed_ok, order, total)
     ordered = jnp.concatenate(
         [neighbors[:CENTRE], neighbors[CENTRE + 1 :], neighbors[CENTRE : CENTRE + 1]], axis=0
     )
     digits = jnp.concatenate([ordered // 64, ordered % 64], axis=0).astype(jnp.bfloat16)
     moved = lax.dot_general(
         digits,
-        place_matrix(where_to, total),
+        place_matrix(order, total),
         (((1,), (1,)), ((), ())),
         preferred_element_type=jnp.float32,
     )
     table = (moved[:OFFSETS] * 128 + moved[OFFSETS:] * 2).astype(jnp.int32)
-    hidden = conv_rows(table, extended, conv_weight, conv_bias, cpe_gain, cpe_bias)
-    got = swap(hidden, num_peers)
+
+    def lay(lines):
+        return jnp.dot(
+            (lines[:, None] == got_slots[None, :]).astype(jnp.bfloat16),
+            got_rows,
+            preferred_element_type=jnp.float32,
+        ).astype(jnp.bfloat16)
+
+    up = [(i, i + 1) for i in range(num_peers - 1)]
+    down = [(i + 1, i) for i in range(num_peers - 1)]
+    before = lax.ppermute(lay(jnp.arange(OWN_CAP - HALO, OWN_CAP)), "pts", up)
+    after = lax.ppermute(lay(jnp.arange(HALO)), "pts", down)
+    extended = jnp.concatenate([before, lay(jnp.arange(OWN_CAP)), after], axis=0)
+
+    weights = (conv_weight, conv_bias, cpe_gain, cpe_bias)
+    first = conv_rows(table[:, :count_first], extended, *weights)
+    first, later = lax.optimization_barrier((first, table[:, count_first:]))
+    first = swap(first, num_peers)
+    last = swap(conv_rows(later, extended, *weights), num_peers)
     return attend_rows(
-        got, got_spots, norm_gain, norm_bias, qkv_weight, qkv_bias, proj_weight, proj_bias,
-        local_rows,
+        first, last, first_spots, last_spots, norm_gain, norm_bias, qkv_weight, qkv_bias,
+        proj_weight, proj_bias, local_rows,
     )
 
 

time: 204 us -> 189 us (0.926)
  blocking collectives: 0 us -> 29.6 us
  Pallas kernels: 106 us -> 85.2 us
  starting transfers between devices: 23.4 us -> 10.3 us
  waiting for transfers between devices: 52.8 us -> 42.1 us
    all_to_all x0 -> x2, blocking collectives: none -> 29.6 us  [the longest x1 17.8 us: swap(): lax.all_to_all(values.reshape((num_peers, -1) + values.shape[1:]), 'pts',...]
    pallas_call x1, Pallas kernels: 51.6 us -> 29.6 us  [attend_rows(): pl.pallas_call(attend_kernel, out_shape=jax.ShapeDtypeStruct((rows, width...]
    all_to_all x4 -> x2, starting transfers between devices: 20 us -> 7.32 us  [swap(): lax.all_to_all(values.reshape((num_peers, -1) + values.shape[1:]), 'pts',...]
    all_to_all x4 -> x2, waiting for transfers between devices: 50.5 us -> 42.1 us  [swap(): lax.all_to_all(values.reshape((num_peers, -1) + values.shape[1:]), 'pts',...]
    ppermute x2, waiting for transfers between devices: 2.27 us -> 0.01 us  [the longest x1 0.01 us: body(): after = lax.ppermute(lay(jnp.arange(HALO)), 'pts', down)]
    pallas_call x1 -> x2, Pallas kernels: 54.2 us -> 55.6 us  [conv_rows(): pl.pallas_call(functools.partial(conv_kernel, block), grid=(steps,), out_...]
    dot_general x2 -> x4, matrix products: 6.72 us -> 7.41 us  [the longest x3 3.99 us: lay(): jnp.dot((lines[:, None] == got_slots[None, :]).astype(jnp.bfloat16), got_...]
  transfers between devices with their start and end apart: 6 -> 4, of which waited for: 4 -> 2; matrix products, arithmetic and copies ran while one was open for 7% -> 4% of each run, Pallas kernels for 27% -> 0%
where the time goes in v2:
time: 189 us
  Pallas kernels  85.2 us (45%)
  waiting for transfers between devices  42.1 us (22%)
  blocking collectives  29.6 us (16%)
  matrix products  12 us (6%)
  starting transfers between devices  10.3 us (5%)
  other arithmetic  4.83 us (3%)
  local copies, waits for them, and re-layouts  4.05 us (2%)
    pallas_call x2, Pallas kernels, conv_rows(): pl.pallas_call(functools.partial(conv_kernel, block), grid=(steps,), out_...  55.6 us
    all_to_all x2, waiting for transfers between devices, swap(): lax.all_to_all(values.reshape((num_peers, -1) + values.shape[1:]), 'pts',...  42.1 us
    pallas_call x1, Pallas kernels, attend_rows(): pl.pallas_call(attend_kernel, out_shape=jax.ShapeDtypeStruct((rows, width...  29.6 us
    all_to_all x1, blocking collectives, swap(): lax.all_to_all(values.reshape((num_peers, -1) + values.shape[1:]), 'pts',...  17.8 us
    all_to_all x1, blocking collectives, body(): lax.all_to_all(jnp.concatenate([slots.reshape(num_peers, send_cap), spots...  11.8 us
    all_to_all x2, starting transfers between devices, swap(): lax.all_to_all(values.reshape((num_peers, -1) + values.shape[1:]), 'pts',...  7.32 us
    dot_general x3, matrix products, lay(): jnp.dot((lines[:, None] == got_slots[None, :]).astype(jnp.bfloat16), got_...  3.99 us
  transfers between devices with their start and end apart: 4, of which 2 were waited for; matrix products, arithmetic and copies ran while one was open for 4% of the time, Pallas kernels for 0%

profile of v2, /device:TPU:0, one launch (start us, length us, event | category | flops | bytes accessed | tf_op | source)
XLA Modules:
  0.0 188.6 jit_solution(17023681013859333856)
XLA Ops:
  0.0 0.8 add_select_fusion.6
  0.8 0.5 fusion.14
  1.2 0.7 fusion.35
  1.9 0.0 copy-start.13
  2.0 2.7 %fusion.8 = bf16[2176,256]{1,0:T(8,128)(2,1)} fusion(bf16[1024,256]{1,0:T(8,128)(2,1)S(1)} %copy-done, s32[1024]{0:T(1024)S(1)} %get-tuple-element.11), kind=kOutput, calls=%fused_computation.17 | convolution fusion | flops 1143635968 | bytes 1642496 | tf_op jit(solution)/shard_map/dot_general | solution.py:54
  4.7 1.4 fusion.11
  6.1 0.0 copy-start.12
  6.2 1.8 select_reduce_fusion
  8.0 0.1 add.94
  8.1 1.0 select_reduce_fusion.1
  9.1 0.1 add.89
  9.2 0.1 pad_add_fusion.1
  9.3 11.8 %all_to_all.27 = s32[8,1,544]{2,1,0:T(1,128)S(1)} all-to-all(s32[8,1,544]{2,1,0:T(1,128)S(1)} %all_to_all.17), channel_id=1, replica_groups=mesh['dp'=4,'pts'=8] {'pts'}, dimensions={0} | all-to-all | bytes 34816 | tf_op jit(solution)/shard_map/all_to_all | solution.py:266
  21.1 3.6 %all-to-all-start.1 = ((bf16[8,272,256]{2,1,0:T(8,128)(2,1)}), bf16[8,272,256]{2,1,0:T(8,128)(2,1)S(1)}, u32[]{:S(2)}, u32[]{:S(2)}) async-start(bf16[8,272,256]{2,1,0:T(8,128)(2,1)} %bitcast.1), calls=%async_computation.1 | async-start | bytes 2228224 | tf_op jit(solution)/shard_map/all_to_all | solution.py:65
  24.7 0.3 fusion.20
  25.0 3.4 %fusion.1 = f32[54,2176]{1,0:T(8,128)S(1)} fusion(s32[2048]{0:T(1024)S(1)} %get-tuple-element.22, bf16[27,2048]{1,0:T(8,128)(2,1)S(1)} %get-tuple-element.18, bf16[27,2048]{1,0:T(8,128)(2,1)S(1)} %get-tuple-element.17), kind=kOutput, calls=%fused_computation.5 | convolution fusion | flops 486195200 | bytes 699392 | tf_op jit(solution)/shard_map/dot_general | solution.py:289
  28.4 0.1 fusion.19
  28.5 0.0 copy-start.10
  28.5 0.2 reshape.50
  28.7 0.2 reshape.58.table_ref
  29.0 0.1 eq.142
  29.1 23.5 %all-to-all-done.1 = bf16[8,272,256]{2,1,0:T(8,128)(2,1)S(1)} async-done(((bf16[8,272,256]{2,1,0:T(8,128)(2,1)}), bf16[8,272,256]{2,1,0:T(8,128)(2,1)S(1)}, u32[]{:S(2)}, u32[]{:S(2)}) %all-to-all-start.1) | async-done | bytes 1114144 | tf_op jit(solution)/shard_map/all_to_all | solution.py:65
  52.6 0.3 convolution_convert_fusion
  52.9 0.4 convolution_convert_fusion.1
  53.3 1.5 collective-permute-start
  54.8 1.5 collective-permute-start.1
  56.3 0.0 copy-start.5
  56.3 3.3 %fusion.9 = bf16[2048,256]{1,0:T(8,128)(2,1)S(1)} fusion(bf16[2176,256]{1,0:T(8,128)(2,1)S(1)} %bitcast.38, s32[2176]{0:T(1024)S(1)} %eq.142), kind=kOutput, calls=%fused_computation.18 | convolution fusion | flops 2286682112 | bytes 2171392 | tf_op jit(solution)/shard_map/dot_general | solution.py:298
  59.6 0.0 copy-start.7
  59.7 0.0 copy-start.8
  59.7 0.1 pad_maximum_fusion.ext_ref
  59.8 0.5 copy-done.7
  60.3 0.0 copy-done.8
  60.3 0.0 copy-done.9
  60.4 35.6 %shard_map.136 = bf16[1408,256]{1,0:T(8,128)(2,1)} custom-call(s32[2,1,19008]{2,1,0:T(1,128)S(1)} %reshape.58.table_ref, bf16[2304,256]{1,0:T(8,128)(2,1)S(1)} %pad_maximum_fusion.ext_ref, bf16[27,256,256]{2,1,0:T(8,128)(2,1)S(1)} %copy-done.5, f32[1,256]{1,0:T(1,128)S(1)} %bitcast.30, f32[1,256]{1,0:T(1,128)S(1)} %bitcast.32, f32[1,256]{1,0:T(1,128)S(1)} %bitcast.34), custom_call_target="tpu_custom_call" | custom-call | flops 4982833152 | bytes 4980736 | tf_op jit(solution)/shard_map/pallas_call | solution.py:135
  95.9 0.1 reshape_transpose_reshape.3.table_ref
  96.0 2.0 %copy-done.6 = bf16[27,256,256]{2,1,0:T(8,128)(2,1)S(1)} copy-done((bf16[27,256,256]{2,1,0:T(8,128)(2,1)S(1)}, bf16[27,256,256]{2,1,0:T(8,128)(2,1)}, u32[]{:S(2)}) %copy-start.6) | copy-done | bytes 3538968
  98.0 20.0 %shard_map.137 = bf16[768,256]{1,0:T(8,128)(2,1)S(1)} custom-call(s32[1,1,20736]{2,1,0:T(1,128)S(1)} %reshape_transpose_reshape.3.table_ref, bf16[2304,256]{1,0:T(8,128)(2,1)S(1)} %pad_maximum_fusion.ext_ref, bf16[27,256,256]{2,1,0:T(8,128)(2,1)S(1)} %copy-done.6, f32[1,256]{1,0:T(1,128)S(1)} %bitcast.31, f32[1,256]{1,0:T(1,128)S(1)} %bitcast.33, ...), custom_call_target="tpu_custom_call" | custom-call | flops 2717908992 | bytes 4325376 | tf_op jit(solution)/shard_map/pallas_call | solution.py:135
  118.1 17.8 %all_to_all.28 = bf16[8,96,256]{2,1,0:T(8,128)(2,1)S(1)} all-to-all(bf16[8,96,256]{2,1,0:T(8,128)(2,1)S(1)} %bitcast.26), channel_id=1, replica_groups=mesh['dp'=4,'pts'=8] {'pts'}, dimensions={0} | all-to-all | bytes 786432 | tf_op jit(solution)/shard_map/all_to_all | solution.py:65
  135.9 3.8 %all-to-all-start.2 = ((bf16[8,176,256]{2,1,0:T(8,128)(2,1)}), bf16[8,176,256]{2,1,0:T(8,128)(2,1)S(1)}, u32[]{:S(2)}, u32[]{:S(2)}) async-start(bf16[8,176,256]{2,1,0:T(8,128)(2,1)} %bitcast.6), calls=%async_computation.2 | async-start | bytes 1441792 | tf_op jit(solution)/shard_map/all_to_all | solution.py:65
  139.7 0.2 copy.27
  139.9 0.2 broadcast_in_dim.91.qkv_bias_ref
  140.0 0.1 slice.45
  140.1 0.1 slice.46
  140.2 0.1 broadcast_in_dim_reshape.4.first_spots_ref
  140.3 0.1 broadcast_in_dim_reshape.10.last_spots_ref
  140.4 18.6 %all-to-all-done.2 = bf16[8,176,256]{2,1,0:T(8,128)(2,1)S(1)} async-done(((bf16[8,176,256]{2,1,0:T(8,128)(2,1)}), bf16[8,176,256]{2,1,0:T(8,128)(2,1)S(1)}, u32[]{:S(2)}, u32[]{:S(2)}) %all-to-all-start.2) | async-done | bytes 720928 | tf_op jit(solution)/shard_map/all_to_all | solution.py:65
  159.0 29.6 %shard_map.138 = bf16[1024,256]{1,0:T(8,128)(2,1)} custom-call(bf16[1408,256]{1,0:T(8,128)(2,1)S(1)} %bitcast.23, bf16[768,256]{1,0:T(8,128)(2,1)S(1)} %bitcast.24, s32[1,1408]{1,0:T(1,128)S(1)} %broadcast_in_dim_reshape.4.first_spots_ref, s32[1,768]{1,0:T(1,128)S(1)} %broadcast_in_dim_reshape.10.last_spots_ref, f32[1,256]{1,0:T(1,128)S(1)} %bitcast.27, ...), custom_call_target="tpu_custom_call" | custom-call | tf_op jit(solution)/shard_map/pallas_call | solution.py:212
  (36 shorter events, 0.2 us)
Async XLA Ops:
  0.0 1.9 %copy-start = (bf16[1024,256]{1,0:T(8,128)(2,1)S(1)}, bf16[1024,256]{1,0:T(8,128)(2,1)}, u32[]{:S(2)}) copy-start(bf16[1024,256]{1,0:T(8,128)(2,1)} %param.14) | copy-start | bytes 1572868
  1.9 2.8 %copy-start.13 = (s32[2048]{0:T(1024)S(1)}, s32[2048]{0:T(1024)}, u32[]{:S(2)}) copy-start(s32[2048]{0:T(1024)} %param.17) | copy-start | bytes 24580
  6.1 18.5 %copy-start.12 = (s32[27,2048]{1,0:T(8,128)S(1)}, s32[27,2048]{1,0:T(8,128)}, u32[]{:S(2)}) copy-start(s32[27,2048]{1,0:T(8,128)} %param.16) | copy-start | bytes 663556
  21.1 31.5 %all-to-all-start.1 = ((bf16[8,272,256]{2,1,0:T(8,128)(2,1)}), bf16[8,272,256]{2,1,0:T(8,128)(2,1)S(1)}, u32[]{:S(2)}, u32[]{:S(2)}) async-start(bf16[8,272,256]{2,1,0:T(8,128)(2,1)} %bitcast.1), calls=%async_computation.1 | async-start | bytes 2228224 | tf_op jit(solution)/shard_map/all_to_all | solution.py:65
  28.5 31.1 %copy-start.10 = (s32[27,2176]{1,0:T(8,128)}, s32[27,2176]{1,0:T(8,128)S(1)}, u32[]{:S(2)}) copy-start(s32[27,2176]{1,0:T(8,128)S(1)} %fusion.19) | copy-start | bytes 705028
  53.3 6.4 %collective-permute-start = (bf16[128,256]{1,0:T(8,128)(2,1)S(1)}, bf16[128,256]{1,0:T(8,128)(2,1)S(1)}, u32[]{:S(2)}, u32[]{:S(2)}) collective-permute-start(bf16[128,256]{1,0:T(8,128)(2,1)S(1)} %convolution_convert_fusion.1), channel_id=1, source_target_pairs={{0,1},{1,2},{2,3},{3,4},{4,5},{5,6},{6,7},{8,9},{9,10},{10,11},{11... | collective-permute-start | bytes 196616 | tf_op jit(solution)/shard_map/ppermute | solution.py:306
  54.8 4.8 %collective-permute-start.1 = (bf16[128,256]{1,0:T(8,128)(2,1)S(1)}, bf16[128,256]{1,0:T(8,128)(2,1)S(1)}, u32[]{:S(2)}, u32[]{:S(2)}) collective-permute-start(bf16[128,256]{1,0:T(8,128)(2,1)S(1)} %convolution_convert_fusion), channel_id=1, source_target_pairs={{1,0},{2,1},{3,2},{4,3},{5,4},{6,5},{7,6},{9,8},{10,9},{11,10},{12... | collective-permute-start | bytes 196616 | tf_op jit(solution)/shard_map/ppermute | solution.py:307
  56.3 3.5 %copy-start.5 = (bf16[27,256,256]{2,1,0:T(8,128)(2,1)S(1)}, bf16[27,256,256]{2,1,0:T(8,128)(2,1)}, u32[]{:S(2)}) copy-start(bf16[27,256,256]{2,1,0:T(8,128)(2,1)} %weight_ref.3) | copy-start | bytes 10616836
  59.6 0.7 copy-start.7
  59.7 0.7 copy-start.8
  59.7 0.7 copy-start.9
  60.4 35.6 %slice-start = ((s32[27,2176]{1,0:T(8,128)}), s32[27,768]{1,0:T(8,128)S(1)}, s32[]{:S(2)}) async-start(s32[27,2176]{1,0:T(8,128)} %copy-done.10), calls=%async_computation.4 | async-start | bytes 196608 | tf_op jit(solution)/shard_map/slice | solution.py:312
  96.0 2.0 %copy-start.6 = (bf16[27,256,256]{2,1,0:T(8,128)(2,1)S(1)}, bf16[27,256,256]{2,1,0:T(8,128)(2,1)}, u32[]{:S(2)}) copy-start(bf16[27,256,256]{2,1,0:T(8,128)(2,1)} %weight_ref.3) | copy-start | bytes 10616836
  118.0 21.6 %copy-start.11 = (bf16[256,768]{1,0:T(8,128)(2,1)S(1)}, bf16[256,768]{1,0:T(8,128)(2,1)}, u32[]{:S(2)}) copy-start(bf16[256,768]{1,0:T(8,128)(2,1)} %param.24) | copy-start | bytes 1179652
  118.1 21.8 %copy-start.14 = (f32[768]{0:T(1024)S(1)}, f32[768]{0:T(1024)}, u32[]{:S(2)}) copy-start(f32[768]{0:T(1024)} %param.25) | copy-start | bytes 9220
  118.1 40.9 %copy-start.1 = (bf16[256,256]{1,0:T(8,128)(2,1)S(1)}, bf16[256,256]{1,0:T(8,128)(2,1)}, u32[]{:S(2)}) copy-start(bf16[256,256]{1,0:T(8,128)(2,1)} %proj_ref.1) | copy-start | bytes 393220
  118.1 40.9 %copy-start.2 = (f32[256]{0:T(256)S(1)}, f32[256]{0:T(256)}, u32[]{:S(2)}) copy-start(f32[256]{0:T(256)} %param.22) | copy-start | bytes 3076
  118.1 40.9 %copy-start.3 = (f32[256]{0:T(256)S(1)}, f32[256]{0:T(256)}, u32[]{:S(2)}) copy-start(f32[256]{0:T(256)} %param.23) | copy-start | bytes 3076
  118.1 40.9 %copy-start.4 = (f32[256]{0:T(256)S(1)}, f32[256]{0:T(256)}, u32[]{:S(2)}) copy-start(f32[256]{0:T(256)} %param.27) | copy-start | bytes 3076
  135.9 23.0 %all-to-all-start.2 = ((bf16[8,176,256]{2,1,0:T(8,128)(2,1)}), bf16[8,176,256]{2,1,0:T(8,128)(2,1)S(1)}, u32[]{:S(2)}, u32[]{:S(2)}) async-start(bf16[8,176,256]{2,1,0:T(8,128)(2,1)} %bitcast.6), calls=%async_computation.2 | async-start | bytes 1441792 | tf_op jit(solution)/shard_map/all_to_all | solution.py:65

commit v3 on v2

--- a/solution.py
+++ b/solution.py
@@ -15,8 +15,7 @@
 HALO = 128
 OFFSETS = 27
 CENTRE = 13
-CONV_BLOCK = 768
-FIRST_SHARE = (22, 34)
+CONV_BLOCK = 1088
 LANES = 128
 ROW_BLOCK = 256
 
@@ -158,17 +157,15 @@
 
 
 def attend_kernel(
-    first_ref, last_ref, first_spots_ref, last_spots_ref, gain_ref, shift_ref, qkv_ref, qkv_bias_ref,
+    got_ref, spots_ref, gain_ref, shift_ref, qkv_ref, qkv_bias_ref,
     proj_ref, proj_bias_ref, out_ref, placed_ref, heads_ref, attended_ref,
 ):
     rows, width = out_ref.shape
     size = ROW_BLOCK
     for start in range(0, rows, size):
         line = lax.broadcasted_iota(jnp.int32, (size, 1), 0) + start
-        placed = 0.0
-        for got_ref, spots_ref in ((first_ref, first_spots_ref), (last_ref, last_spots_ref)):
-            match = jnp.where(spots_ref[...] == line, 1.0, 0.0).astype(jnp.bfloat16)
-            placed += jnp.dot(match, got_ref[...], preferred_element_type=jnp.float32)
+        match = jnp.where(spots_ref[...] == line, 1.0, 0.0).astype(jnp.bfloat16)
+        placed = jnp.dot(match, got_ref[...], preferred_element_type=jnp.float32)
         placed_ref[pl.ds(start, size), :] = placed
         normed = layer_norm(placed, gain_ref[...], shift_ref[...]).astype(jnp.bfloat16)
         product = lax.dot_general(
@@ -205,14 +202,13 @@
 
 
 def attend_rows(
-    first, last, first_spots, last_spots, norm_gain, norm_bias, qkv_weight, qkv_bias,
-    proj_weight, proj_bias, rows,
+    got, spots, norm_gain, norm_bias, qkv_weight, qkv_bias, proj_weight, proj_bias, rows
 ):
-    width = first.shape[1]
+    width = got.shape[1]
     return pl.pallas_call(
         attend_kernel,
         out_shape=jax.ShapeDtypeStruct((rows, width), jnp.bfloat16),
-        in_specs=[pl.BlockSpec(memory_space=pltpu.VMEM)] * 10,
+        in_specs=[pl.BlockSpec(memory_space=pltpu.VMEM)] * 8,
         out_specs=pl.BlockSpec(memory_space=pltpu.VMEM),
         scratch_shapes=[
             pltpu.VMEM((rows, width), jnp.float32),
@@ -221,7 +217,7 @@
         ],
         compiler_params=pltpu.CompilerParams(vmem_limit_bytes=50 * 2**20),
     )(
-        first, last, first_spots[None, :], last_spots[None, :], norm_gain[None, :], norm_bias[None, :], qkv_weight.T,
+        got, spots[None, :], norm_gain[None, :], norm_bias[None, :], qkv_weight.T,
         qkv_bias[:, None], proj_weight, proj_bias[None, :],
     )
 
@@ -249,19 +245,12 @@
 
     owners = tile_slot // OWN_CAP
     where_to = buffer_index(owners, jnp.ones(owners.shape, bool), num_peers, send_cap, total)
-    packed, serial, where_in = lax.optimization_barrier(
-        (place_rows(where_to, features, total), serial, where_to)
-    )
-    got_rows = swap(packed, num_peers)
-    slots = place_numbers(where_in, tile_slot % OWN_CAP, OWN_CAP, total)
-
-    cap_first = send_cap * FIRST_SHARE[0] // FIRST_SHARE[1]
-    cap_last = send_cap - cap_first
-    count_first = num_peers * cap_first
+    got_rows = swap(place_rows(where_to, features, total), num_peers)
+    slots = place_numbers(where_to, tile_slot % OWN_CAP, OWN_CAP, total)
+
     placed_ok = serial >= 0
     devices_to = jnp.where(placed_ok, serial // PTS_DEV, 0)
-    ranking = arrival_rank(devices_to, placed_ok, num_peers)
-    where_to = jnp.where(placed_ok, devices_to * send_cap + ranking, total)
+    where_to = buffer_index(devices_to, placed_ok, num_peers, send_cap, total)
     spots = place_numbers(where_to, serial % PTS_DEV, PTS_DEV, total)
     numbers = lax.all_to_all(
         jnp.concatenate(
@@ -273,22 +262,14 @@
         tiled=True,
     )
     got_slots = numbers[:, :send_cap].reshape(-1)
-    first_spots = numbers[:, send_cap : send_cap + cap_first].reshape(-1)
-    last_spots = numbers[:, send_cap + cap_first :].reshape(-1)
-
-    order = jnp.where(
-        ranking < cap_first,
-        devices_to * cap_first + ranking,
-        count_first + devices_to * cap_last + ranking - cap_first,
-    )
-    order = jnp.where(placed_ok, order, total)
+    got_spots = numbers[:, send_cap:].reshape(-1)
     ordered = jnp.concatenate(
         [neighbors[:CENTRE], neighbors[CENTRE + 1 :], neighbors[CENTRE : CENTRE + 1]], axis=0
     )
     digits = jnp.concatenate([ordered // 64, ordered % 64], axis=0).astype(jnp.bfloat16)
     moved = lax.dot_general(
         digits,
-        place_matrix(order, total),
+        place_matrix(where_to, total),
         (((1,), (1,)), ((), ())),
         preferred_element_type=jnp.float32,
     )
@@ -307,14 +288,11 @@
     after = lax.ppermute(lay(jnp.arange(HALO)), "pts", down)
     extended = jnp.concatenate([before, lay(jnp.arange(OWN_CAP)), after], axis=0)
 
-    weights = (conv_weight, conv_bias, cpe_gain, cpe_bias)
-    first = conv_rows(table[:, :count_first], extended, *weights)
-    first, later = lax.optimization_barrier((first, table[:, count_first:]))
-    first = swap(first, num_peers)
-    last = swap(conv_rows(later, extended, *weights), num_peers)
+    hidden = conv_rows(table, extended, conv_weight, conv_bias, cpe_gain, cpe_bias)
+    got = swap(hidden, num_peers)
     return attend_rows(
-        first, last, first_spots, last_spots, norm_gain, norm_bias, qkv_weight, qkv_bias,
-        proj_weight, proj_bias, local_rows,
+        got, got_spots, norm_gain, norm_bias, qkv_weight, qkv_bias, proj_weight, proj_bias,
+        local_rows,
     )
 
 

time: 189 us -> 175 us (0.926)
  blocking collectives: 29.6 us -> 0 us
  waiting for transfers between devices: 42.1 us -> 53.8 us
  starting transfers between devices: 10.3 us -> 18.8 us
  Pallas kernels: 85.2 us -> 83.3 us
    all_to_all x2 -> x0, blocking collectives: 29.6 us -> none  [the longest x1 17.8 us: swap(): lax.all_to_all(values.reshape((num_peers, -1) + values.shape[1:]), 'pts',...]
    all_to_all x2, waiting for transfers between devices: 42.1 us -> 50.9 us  [swap(): lax.all_to_all(values.reshape((num_peers, -1) + values.shape[1:]), 'pts',...]
    all_to_all x0 -> x1, starting transfers between devices: none -> 6.33 us  [body(): lax.all_to_all(jnp.concatenate([slots.reshape(num_peers, send_cap), spots...]
    all_to_all x0 -> x1, waiting for transfers between devices: none -> 2.9 us  [body(): lax.all_to_all(jnp.concatenate([slots.reshape(num_peers, send_cap), spots...]
    all_to_all x2, starting transfers between devices: 7.32 us -> 9.42 us  [swap(): lax.all_to_all(values.reshape((num_peers, -1) + values.shape[1:]), 'pts',...]
    unnamed x32 -> x30, local copies, waits for them, and re-layouts: 2.81 us -> 0.8 us
    pallas_call x2 -> x1, Pallas kernels: 55.6 us -> 53.6 us  [conv_rows(): pl.pallas_call(functools.partial(conv_kernel, block), grid=(steps,), out_...]
  transfers between devices with their start and end apart: 4 -> 5, of which waited for: 2 -> 3; matrix products, arithmetic and copies ran while one was open for 4% -> 6% of each run, Pallas kernels for 0% -> 0%
where the time goes in v3:
time: 175 us
  Pallas kernels  83.3 us (48%)
  waiting for transfers between devices  53.8 us (31%)
  starting transfers between devices  18.8 us (11%)
  matrix products  12.1 us (7%)
  other arithmetic  4.15 us (2%)
  local copies, waits for them, and re-layouts  2.53 us (1%)
    pallas_call x1, Pallas kernels, conv_rows(): pl.pallas_call(functools.partial(conv_kernel, block), grid=(steps,), out_...  53.6 us
    all_to_all x2, waiting for transfers between devices, swap(): lax.all_to_all(values.reshape((num_peers, -1) + values.shape[1:]), 'pts',...  50.9 us
    pallas_call x1, Pallas kernels, attend_rows(): pl.pallas_call(attend_kernel, out_shape=jax.ShapeDtypeStruct((rows, width...  29.6 us
    all_to_all x2, starting transfers between devices, swap(): lax.all_to_all(values.reshape((num_peers, -1) + values.shape[1:]), 'pts',...  9.42 us
    all_to_all x1, starting transfers between devices, body(): lax.all_to_all(jnp.concatenate([slots.reshape(num_peers, send_cap), spots...  6.33 us
    dot_general x3, matrix products, lay(): jnp.dot((lines[:, None] == got_slots[None, :]).astype(jnp.bfloat16), got_...  4 us
  transfers between devices with their start and end apart: 5, of which 3 were waited for; matrix products, arithmetic and copies ran while one was open for 6% of the time, Pallas kernels for 0%

profile of v3, /device:TPU:0, one launch (start us, length us, event | category | flops | bytes accessed | tf_op | source)
XLA Modules:
  0.0 175.0 jit_solution(10028232750088409242)
XLA Ops:
  0.0 0.8 fusion.31
  0.8 0.0 copy-start.11
  0.8 0.0 copy-start.12
  0.8 1.4 fusion.11
  2.3 1.9 %select_reduce_fusion = s32[2176]{0:T(1024)S(1)} fusion(s32[2048]{0:T(1024)S(1)} %get-tuple-element.13, s32[2048]{0:T(1024)S(1)} %get-tuple-element.14), kind=kLoop, calls=%fused_computation.1 | loop fusion | flops 13367168 | bytes 25088 | tf_op jit(solution)/shard_map/reduce_sum | solution.py:60
  4.1 0.1 add.77
  4.2 0.5 fusion.14
  4.7 1.0 select_reduce_fusion.1
  5.7 0.1 add.73
  5.8 0.1 pad_add_fusion.1
  5.9 0.6 all_to_all.14
  6.5 6.3 %all-to-all-start = ((s32[8,1,544]{2,1,0:T(1,128)}), s32[8,1,544]{2,1,0:T(1,128)S(1)}, u32[]{:S(2)}, u32[]{:S(2)}) async-start(s32[8,1,544]{2,1,0:T(1,128)} %all_to_all.14), calls=%async_computation | async-start | bytes 40960 | tf_op jit(solution)/shard_map/all_to_all | solution.py:255
  12.8 0.0 copy-start.10
  12.9 2.7 %fusion.8 = bf16[2176,256]{1,0:T(8,128)(2,1)} fusion(bf16[1024,256]{1,0:T(8,128)(2,1)S(1)} %copy-done, s32[1024]{0:T(1024)S(1)} %get-tuple-element.16), kind=kOutput, calls=%fused_computation.15 | convolution fusion | flops 1143635968 | bytes 1642496 | tf_op jit(solution)/shard_map/dot_general | solution.py:53
  15.6 2.9 %all-to-all-done = s32[8,1,544]{2,1,0:T(1,128)S(1)} async-done(((s32[8,1,544]{2,1,0:T(1,128)}), s32[8,1,544]{2,1,0:T(1,128)S(1)}, u32[]{:S(2)}, u32[]{:S(2)}) %all-to-all-start) | async-done | bytes 17440 | tf_op jit(solution)/shard_map/all_to_all | solution.py:255
  18.5 3.6 %all-to-all-start.1 = ((bf16[8,272,256]{2,1,0:T(8,128)(2,1)}), bf16[8,272,256]{2,1,0:T(8,128)(2,1)S(1)}, u32[]{:S(2)}, u32[]{:S(2)}) async-start(bf16[8,272,256]{2,1,0:T(8,128)(2,1)} %bitcast.1), calls=%async_computation.1 | async-start | bytes 2228224 | tf_op jit(solution)/shard_map/all_to_all | solution.py:64
  22.1 0.3 fusion.20
  22.4 3.4 %fusion = f32[54,2176]{1,0:T(8,128)S(1)} fusion(s32[2048]{0:T(1024)S(1)} %get-tuple-element.14, bf16[27,2048]{1,0:T(8,128)(2,1)S(1)} %get-tuple-element.8, bf16[27,2048]{1,0:T(8,128)(2,1)S(1)} %get-tuple-element.7), kind=kOutput, calls=%fused_computation.3 | convolution fusion | flops 486195200 | bytes 699392 | tf_op jit(solution)/shard_map/dot_general | solution.py:270
  25.8 0.1 fusion.19
  25.9 0.2 reshape.42
  26.1 0.3 reshape.48.table_ref
  26.4 0.1 fusion.40
  26.5 0.1 eq.61
  26.6 23.4 %all-to-all-done.1 = bf16[8,272,256]{2,1,0:T(8,128)(2,1)S(1)} async-done(((bf16[8,272,256]{2,1,0:T(8,128)(2,1)}), bf16[8,272,256]{2,1,0:T(8,128)(2,1)S(1)}, u32[]{:S(2)}, u32[]{:S(2)}) %all-to-all-start.1) | async-done | bytes 1114144 | tf_op jit(solution)/shard_map/all_to_all | solution.py:64
  50.0 0.3 convolution_convert_fusion
  50.3 0.4 convolution_convert_fusion.1
  50.7 1.5 collective-permute-start
  52.3 1.5 collective-permute-start.1
  53.7 0.0 copy-start.5
  53.8 3.3 %fusion.9 = bf16[2048,256]{1,0:T(8,128)(2,1)S(1)} fusion(bf16[2176,256]{1,0:T(8,128)(2,1)S(1)} %bitcast.32, s32[2176]{0:T(1024)S(1)} %eq.61), kind=kOutput, calls=%fused_computation.16 | convolution fusion | flops 2286682112 | bytes 2171392 | tf_op jit(solution)/shard_map/dot_general | solution.py:279
  57.1 0.0 copy-start.6
  57.1 0.0 copy-start.7
  57.1 0.0 copy-start.8
  57.1 0.0 collective-permute-done
  57.1 0.0 collective-permute-done.1
  57.1 0.1 pad_maximum_fusion.ext_ref
  57.2 0.5 copy-done.6
  57.7 0.0 copy-done.7
  57.8 0.0 copy-done.8
  57.8 53.6 %shard_map.136 = bf16[2176,256]{1,0:T(8,128)(2,1)} custom-call(s32[2,1,29376]{2,1,0:T(1,128)S(1)} %reshape.48.table_ref, bf16[2304,256]{1,0:T(8,128)(2,1)S(1)} %pad_maximum_fusion.ext_ref, bf16[27,256,256]{2,1,0:T(8,128)(2,1)S(1)} %copy-done.5, f32[1,256]{1,0:T(1,128)S(1)} %bitcast.26, f32[1,256]{1,0:T(1,128)S(1)} %bitcast.27, f32[1,256]{1,0:T(1,128)S(1)} %bitcast.28), custom_call_target="tpu_custom_call" | custom-call | flops 7700742144 | bytes 5767168 | tf_op jit(solution)/shard_map/pallas_call | solution.py:134
  111.4 0.0 copy-start.3
  111.4 0.0 copy-start.4
  111.4 5.9 %all-to-all-start.2 = ((bf16[8,272,256]{2,1,0:T(8,128)(2,1)}), bf16[8,272,256]{2,1,0:T(8,128)(2,1)S(1)}, u32[]{:S(2)}, u32[]{:S(2)}) async-start(bf16[8,272,256]{2,1,0:T(8,128)(2,1)} %bitcast.6), calls=%async_computation.2 | async-start | bytes 2228224 | tf_op jit(solution)/shard_map/all_to_all | solution.py:64
  117.3 0.2 copy.27
  117.5 0.2 broadcast_in_dim.87.qkv_bias_ref
  117.6 0.1 broadcast_in_dim_reshape.2.spots_ref
  117.7 27.5 %all-to-all-done.2 = bf16[8,272,256]{2,1,0:T(8,128)(2,1)S(1)} async-done(((bf16[8,272,256]{2,1,0:T(8,128)(2,1)}), bf16[8,272,256]{2,1,0:T(8,128)(2,1)S(1)}, u32[]{:S(2)}, u32[]{:S(2)}) %all-to-all-start.2) | async-done | bytes 1114144 | tf_op jit(solution)/shard_map/all_to_all | solution.py:64
  145.3 29.6 %shard_map.137 = bf16[1024,256]{1,0:T(8,128)(2,1)} custom-call(bf16[2176,256]{1,0:T(8,128)(2,1)S(1)} %bitcast.21, s32[1,2176]{1,0:T(1,128)S(1)} %broadcast_in_dim_reshape.2.spots_ref, f32[1,256]{1,0:T(1,128)S(1)} %bitcast.23, f32[1,256]{1,0:T(1,128)S(1)} %bitcast.24, bf16[768,256]{1,0:T(8,128)(2,1)S(1)} %bitcast.22, ...), custom_call_target="tpu_custom_call" | custom-call | tf_op jit(solution)/shard_map/pallas_call | solution.py:208
  (26 shorter events, 0.1 us)
Async XLA Ops:
  0.0 12.8 %copy-start = (bf16[1024,256]{1,0:T(8,128)(2,1)S(1)}, bf16[1024,256]{1,0:T(8,128)(2,1)}, u32[]{:S(2)}) copy-start(bf16[1024,256]{1,0:T(8,128)(2,1)} %param.14) | copy-start | bytes 1572868
  0.8 1.5 copy-start.11
  0.8 3.4 %copy-start.12 = (s32[1024]{0:T(1024)S(1)}, s32[1024]{0:T(1024)}, u32[]{:S(2)}) copy-start(s32[1024]{0:T(1024)} %param.15) | copy-start | bytes 12292
  6.5 12.0 %all-to-all-start = ((s32[8,1,544]{2,1,0:T(1,128)}), s32[8,1,544]{2,1,0:T(1,128)S(1)}, u32[]{:S(2)}, u32[]{:S(2)}) async-start(s32[8,1,544]{2,1,0:T(1,128)} %all_to_all.14), calls=%async_computation | async-start | bytes 40960 | tf_op jit(solution)/shard_map/all_to_all | solution.py:255
  12.8 2.8 %copy-start.10 = (s32[27,2048]{1,0:T(8,128)S(1)}, s32[27,2048]{1,0:T(8,128)}, u32[]{:S(2)}) copy-start(s32[27,2048]{1,0:T(8,128)} %param.16) | copy-start | bytes 663556
  18.5 31.5 %all-to-all-start.1 = ((bf16[8,272,256]{2,1,0:T(8,128)(2,1)}), bf16[8,272,256]{2,1,0:T(8,128)(2,1)S(1)}, u32[]{:S(2)}, u32[]{:S(2)}) async-start(bf16[8,272,256]{2,1,0:T(8,128)(2,1)} %bitcast.1), calls=%async_computation.1 | async-start | bytes 2228224 | tf_op jit(solution)/shard_map/all_to_all | solution.py:64
  50.7 6.4 %collective-permute-start = (bf16[128,256]{1,0:T(8,128)(2,1)S(1)}, bf16[128,256]{1,0:T(8,128)(2,1)S(1)}, u32[]{:S(2)}, u32[]{:S(2)}) collective-permute-start(bf16[128,256]{1,0:T(8,128)(2,1)S(1)} %convolution_convert_fusion.1), channel_id=1, source_target_pairs={{0,1},{1,2},{2,3},{3,4},{4,5},{5,6},{6,7},{8,9},{9,10},{10,11},{11... | collective-permute-start | bytes 196616 | tf_op jit(solution)/shard_map/ppermute | solution.py:287
  52.3 4.9 %collective-permute-start.1 = (bf16[128,256]{1,0:T(8,128)(2,1)S(1)}, bf16[128,256]{1,0:T(8,128)(2,1)S(1)}, u32[]{:S(2)}, u32[]{:S(2)}) collective-permute-start(bf16[128,256]{1,0:T(8,128)(2,1)S(1)} %convolution_convert_fusion), channel_id=1, source_target_pairs={{1,0},{2,1},{3,2},{4,3},{5,4},{6,5},{7,6},{9,8},{10,9},{11,10},{12... | collective-permute-start | bytes 196616 | tf_op jit(solution)/shard_map/ppermute | solution.py:288
  53.7 3.5 %copy-start.5 = (bf16[27,256,256]{2,1,0:T(8,128)(2,1)S(1)}, bf16[27,256,256]{2,1,0:T(8,128)(2,1)}, u32[]{:S(2)}) copy-start(bf16[27,256,256]{2,1,0:T(8,128)(2,1)} %weight_ref.1) | copy-start | bytes 10616836
  57.1 0.7 copy-start.6
  57.1 0.7 copy-start.7
  57.1 0.7 copy-start.8
  111.4 5.9 %copy-start.9 = (bf16[256,768]{1,0:T(8,128)(2,1)S(1)}, bf16[256,768]{1,0:T(8,128)(2,1)}, u32[]{:S(2)}) copy-start(bf16[256,768]{1,0:T(8,128)(2,1)} %param.24) | copy-start | bytes 1179652
  111.4 6.1 %copy-start.13 = (f32[768]{0:T(1024)S(1)}, f32[768]{0:T(1024)}, u32[]{:S(2)}) copy-start(f32[768]{0:T(1024)} %param.25) | copy-start | bytes 9220
  111.4 33.9 %copy-start.1 = (bf16[256,256]{1,0:T(8,128)(2,1)S(1)}, bf16[256,256]{1,0:T(8,128)(2,1)}, u32[]{:S(2)}) copy-start(bf16[256,256]{1,0:T(8,128)(2,1)} %proj_ref.1) | copy-start | bytes 393220
  111.4 33.9 %copy-start.2 = (f32[256]{0:T(256)S(1)}, f32[256]{0:T(256)}, u32[]{:S(2)}) copy-start(f32[256]{0:T(256)} %param.22) | copy-start | bytes 3076
  111.4 33.9 %copy-start.3 = (f32[256]{0:T(256)S(1)}, f32[256]{0:T(256)}, u32[]{:S(2)}) copy-start(f32[256]{0:T(256)} %param.23) | copy-start | bytes 3076
  111.4 33.9 %copy-start.4 = (f32[256]{0:T(256)S(1)}, f32[256]{0:T(256)}, u32[]{:S(2)}) copy-start(f32[256]{0:T(256)} %param.27) | copy-start | bytes 3076
  111.4 33.9 %all-to-all-start.2 = ((bf16[8,272,256]{2,1,0:T(8,128)(2,1)}), bf16[8,272,256]{2,1,0:T(8,128)(2,1)S(1)}, u32[]{:S(2)}, u32[]{:S(2)}) async-start(bf16[8,272,256]{2,1,0:T(8,128)(2,1)} %bitcast.6), calls=%async_computation.2 | async-start | bytes 2228224 | tf_op jit(solution)/shard_map/all_to_all | solution.py:64
